TPU v7x, 512 devices: a whole 4x4x16 slice. The times are simulated.
512 devices in a mesh: dp: 32 (over y, z_lo), tensor: 16 (over x, z_hi, core).
Axes of the slice: x: 4, y: 4, z: 16 (z_hi: 2, z_lo: 8; z = z_hi * 8 + z_lo), core: 2. Of those that a mesh axis runs over, the one named last changes fastest.
Arguments:
- acts: bfloat16 [8192, 8192], P('dp', 'tensor'), may hold values from -6 to 6
- gate_pre: bfloat16 [8192, 28672], P('dp', 'tensor'), may hold values from -9 to 9
- up_pre: bfloat16 [8192, 28672], P('dp', 'tensor'), may hold values from -6 to 6
- hidden_grad: bfloat16 [8192, 28672], P('dp', 'tensor'), may hold values from -6 to 6
- proj_in: bfloat16 [64, 8192], P(None, 'tensor'), may hold values from -0.0625 to 0.0625
- proj_out: bfloat16 [2, 64, 28672], P(None, None, 'tensor'), may hold values from -0.0234375 to 0.0234375
- queries: bfloat16 [65536, 4096], P('dp', 'tensor'), may hold values from -0.019897461 to 0.019897461
Outputs:
- sketches: bfloat16 [64, 4096], P('dp', 'tensor')
- scores: float32 [65536, 64], P(('dp', 'tensor'))
All inputs are finite; a program needn't handle non-finite values.
Results may differ from a plain program's by a relative error of at most 0.0049.
Values may be sent and summed in bfloat16 or wider, within the bound.
No kernel may reach another device: no remote copies, remote signals or barrier semaphores. Data moves between devices by JAX's collectives and lax.ppermute only.
A program may use at most 64 MiB of HBM per device.

v0:
```python
import jax
import jax.numpy as jnp
from jax import lax
from jax.sharding import PartitionSpec as P

SEQ_LEN = 128


def contract(left, right):
    return lax.dot_general(
        left, right, (((1,), (1,)), ((), ())), preferred_element_type=jnp.float32
    )


def per_device(acts, gate_pre, up_pre, hidden_grad, proj_in, proj_out, queries):
    rank = proj_in.shape[0]
    tok_rows = acts.shape[0]
    seq_count = tok_rows // SEQ_LEN
    gate = gate_pre.astype(jnp.float32)
    upval = up_pre.astype(jnp.float32)
    grad = hidden_grad.astype(jnp.float32)
    sig = jax.nn.sigmoid(gate)
    gate_grad = (grad * upval * sig * (1.0 + gate * (1.0 - sig))).astype(jnp.bfloat16)
    up_grad = (grad * gate * sig).astype(jnp.bfloat16)
    part_out = contract(gate_grad, proj_out[0]) + contract(up_grad, proj_out[1])
    part_in = contract(acts, proj_in)
    stacked = jnp.concatenate([part_out, part_in], axis=1)
    width_dev = queries.shape[1]
    summed = lax.psum(stacked, "tensor")
    blocks = summed.reshape(seq_count, SEQ_LEN, 2 * rank)
    outer = jnp.einsum(
        "sta,stb->sab", blocks[:, :, :rank], blocks[:, :, rank:], precision=lax.Precision.HIGHEST
    )
    outer = outer.reshape(seq_count, rank * rank)
    col_start = lax.axis_index("tensor") * width_dev
    own_cols = lax.dynamic_slice_in_dim(outer, col_start, width_dev, 1)
    sketches = own_cols.astype(jnp.bfloat16)
    whole_sketch = lax.all_gather(sketches, "tensor", axis=1, tiled=True)
    train_all = lax.all_gather(whole_sketch, "dp", axis=0, tiled=True)
    own_queries = lax.all_to_all(queries, "tensor", split_axis=0, concat_axis=1, tiled=True)
    scores = contract(own_queries, train_all)
    return (sketches, scores)


def solution(mesh):
    return jax.shard_map(
        per_device,
        mesh=mesh,
        in_specs=(
            P("dp", "tensor"),
            P("dp", "tensor"),
            P("dp", "tensor"),
            P("dp", "tensor"),
            P(None, "tensor"),
            P(None, None, "tensor"),
            P("dp", "tensor"),
        ),
        out_specs=(P("dp", "tensor"), P(("dp", "tensor"), None)),
        check_vma=False,
    )
```

profile of v0, /device:TPU:2, one launch (start us, length us, event | category | flops | bytes accessed | tf_op | source)
XLA Modules:
  0.0 473.5 jit_solution(16408026390903673893)
XLA Ops:
  7.2 0.0 copy-start
  7.2 0.0 copy-start.1
  7.2 18.2 %all-to-all-start = ((bf16[16,128,256]{2,1,0:T(8,128)(2,1)}), bf16[16,128,256]{2,1,0:T(8,128)(2,1)S(1)}, u32[]{:S(2)}, u32[]{:S(2)}) async-start(bf16[16,128,256]{2,1,0:T(8,128)(2,1)} %bitcast.23), calls=%async_computation | async-start | bytes 2097152 | tf_op jit(solution)/shard_map/all_to_all | solution.py:40
  25.5 0.0 all-reduce.2.cloned.1.call-start
  25.5 0.2 fusion.21
  25.7 0.0 copy-start.5
  25.8 0.0 copy-start.6
  25.8 2.2 fusion.10
  28.0 0.0 copy-done.5
  28.0 0.0 copy-done.6
  28.0 0.7 convolution_add_fusion
  28.7 0.7 copy_bitcast_fusion
  29.4 0.0 all-reduce.2.cloned.1.call-update
  29.4 265.6 %all-reduce.2.cloned.1.call-done = f32[2,128,128]{1,2,0:T(8,128)} async-done(((f32[2,128,128]{1,2,0:T(8,128)}), f32[2,128,128]{1,2,0:T(8,128)}) %all-reduce.2.cloned.1.call-update) | async-done | bytes 131088 | tf_op jit(solution)/shard_map/psum | solution.py:29
  295.0 1.1 fusion.16
  296.1 0.1 reshape.14
  296.2 0.0 copy-start.2
  296.2 49.5 %all_gather.6 = bf16[2,4096]{1,0:T(2,128)(2,1)S(1)} all-gather(bf16[2,256]{1,0:T(2,128)(2,1)S(1)} %dynamic-slice_convert_fusion), channel_id=1, replica_groups=mesh['dp'=32,'tensor'=16] {'tensor'}, dimensions={1}, use_global_device_ids=true | all-gather | bytes 17408 | tf_op jit(solution)/shard_map/all_gather | solution.py:38
  345.8 119.0 %all-gather = bf16[32,2,4096]{2,1,0:T(2,128)(2,1)S(1)} all-gather(bf16[1,2,4096]{2,1,0:T(2,128)(2,1)S(1)} %bitcast.24), channel_id=1, replica_groups=mesh['dp'=32,'tensor'=16] {'dp'}, dimensions={0}, use_global_device_ids=true | all-gather | bytes 540672 | tf_op jit(solution)/shard_map/all_gather | solution.py:39
  464.8 0.2 reshape.16
  465.0 0.0 all-to-all-done
  465.0 0.7 copy.14
  465.7 0.0 copy-done.2
  465.7 0.9 convolution_bitcast_fusion
  (7 shorter events, 0.0 us)
Async XLA Ops:
  7.2 18.3 %copy-start = (bf16[256,512]{1,0:T(8,128)(2,1)S(1)}, bf16[256,512]{1,0:T(8,128)(2,1)}, u32[]{:S(2)}) copy-start(bf16[256,512]{1,0:T(8,128)(2,1)} %param.7) | copy-start | bytes 786436
  7.2 18.3 %copy-start.1 = (bf16[64,512]{1,0:T(8,128)(2,1)S(1)}, bf16[64,512]{1,0:T(8,128)(2,1)}, u32[]{:S(2)}) copy-start(bf16[64,512]{1,0:T(8,128)(2,1)} %param.11) | copy-start | bytes 196612
  7.2 18.5 %copy-start.3 = (bf16[256,1792]{1,0:T(8,128)(2,1)S(1)}, bf16[256,1792]{1,0:T(8,128)(2,1)}, u32[]{:S(2)}) copy-start(bf16[256,1792]{1,0:T(8,128)(2,1)} %param.9) | copy-start | bytes 2752516
  7.2 18.5 %copy-start.4 = (bf16[256,1792]{1,0:T(8,128)(2,1)S(1)}, bf16[256,1792]{1,0:T(8,128)(2,1)}, u32[]{:S(2)}) copy-start(bf16[256,1792]{1,0:T(8,128)(2,1)} %param.10) | copy-start | bytes 2752516
  7.2 457.8 %all-to-all-start = ((bf16[16,128,256]{2,1,0:T(8,128)(2,1)}), bf16[16,128,256]{2,1,0:T(8,128)(2,1)S(1)}, u32[]{:S(2)}, u32[]{:S(2)}) async-start(bf16[16,128,256]{2,1,0:T(8,128)(2,1)} %bitcast.23), calls=%async_computation | async-start | bytes 2097152 | tf_op jit(solution)/shard_map/all_to_all | solution.py:40
  25.5 269.5 %all-reduce.2.cloned.1.call-start = ((), (), s32[]{:S(2)}) async-start(), calls=%async_computation.1 | async-start | bytes 262144 | tf_op jit(solution)/shard_map/psum | solution.py:29
  25.7 2.3 copy-start.5
  25.8 2.3 copy-start.6
  296.2 169.5 %copy-start.2 = (bf16[2,256]{1,0:T(2,128)(2,1)}, bf16[2,256]{1,0:T(2,128)(2,1)S(1)}, u32[]{:S(2)}) copy-start(bf16[2,256]{1,0:T(2,128)(2,1)S(1)} %dynamic-slice_convert_fusion) | copy-start | bytes 3076
Sparse Core Ops, SparseCore 0:
  29.5 265.4 all-reduce.1
where the time goes:
time: 474 us; the launch traced here: 473 us
  waiting for transfers between devices  266 us (56%)
  blocking collectives  169 us (36%)
  starting transfers between devices  18.3 us (4%)
  between operations  14.2 us (3%)
  matrix products  5.13 us (1%)
    psum x1, waiting for transfers between devices, per_device(): summed = lax.psum(stacked, 'tensor')  266 us
    all_gather x1, blocking collectives, per_device(): train_all = lax.all_gather(whole_sketch, 'dp', axis=0, tiled=True)  119 us
    all_gather x1, blocking collectives, per_device(): whole_sketch = lax.all_gather(sketches, 'tensor', axis=1, tiled=True)  49.5 us
    all_to_all x1, starting transfers between devices, per_device(): lax.all_to_all(queries, 'tensor', split_axis=0, concat_axis=1, tiled=True)  18.2 us
  transfers between devices with their start and end apart: 2, of which 1 were waited for; matrix products, arithmetic and copies ran while one was open for 1% of the time, Pallas kernels for 0%

commit v1 on v0

v1 whole, which is shorter than its diff:
```python
import jax
import jax.numpy as jnp
from jax import lax
from jax.sharding import Mesh, PartitionSpec as P

SEQ_LEN = 128
COLS = ("pair", "core")


def contract(left, right):
    return lax.dot_general(
        left, right, (((1,), (1,)), ((), ())), preferred_element_type=jnp.float32
    )


def exchange(blocks, axes):
    return lax.all_to_all(blocks, axes, split_axis=0, concat_axis=0, tiled=False)


def per_device(acts, gate_pre, up_pre, hidden_grad, proj_in, proj_out, queries):
    rank = proj_in.shape[0]
    tok = acts.shape[0]
    seqs = tok // SEQ_LEN
    n_dp, n_pair = lax.axis_size("dp"), lax.axis_size("pair")
    wide = rank // n_pair
    half = rank // 2
    gate = gate_pre.astype(jnp.float32)
    upval = up_pre.astype(jnp.float32)
    grad = hidden_grad.astype(jnp.float32)
    sig = jax.nn.sigmoid(gate)
    gate_grad = (grad * upval * sig * (1.0 + gate * (1.0 - sig))).astype(jnp.bfloat16)
    up_grad = (grad * gate * sig).astype(jnp.bfloat16)
    out_t = contract(proj_out[0], gate_grad) + contract(proj_out[1], up_grad)
    in_t = contract(proj_in, acts)
    out_b = out_t.astype(jnp.bfloat16).reshape(n_pair, 1, wide, tok)
    in_b = in_t.astype(jnp.bfloat16).reshape(1, 2, half, tok)
    parts = jnp.concatenate(
        [
            jnp.broadcast_to(out_b, (n_pair, 2, wide, tok)),
            jnp.broadcast_to(in_b, (n_pair, 2, half, tok)),
        ],
        axis=2,
    ).reshape(2 * n_pair, wide + half, tok)
    got = exchange(parts, COLS)
    total = jnp.sum(got.astype(jnp.float32), axis=0)
    outs = total[:wide].reshape(wide, seqs, SEQ_LEN)
    ins = total[wide:].reshape(half, seqs, SEQ_LEN)
    block = jnp.einsum("ast,bst->sab", outs, ins, precision=lax.Precision.HIGHEST)
    block = block.astype(jnp.bfloat16).reshape(seqs, 2, wide // 2 * half)
    sends = jnp.broadcast_to(block.transpose(1, 0, 2), (n_dp, 2, seqs, wide // 2 * half))
    sends = sends.reshape(n_dp * 2, seqs, wide // 2 * half)
    all_blocks = exchange(sends, ("dp", "core"))
    all_blocks = all_blocks.reshape(n_dp, 2, seqs, wide // 2, half)
    train = all_blocks.transpose(0, 2, 3, 1, 4).reshape(n_dp * seqs, wide // 2 * rank)
    sketches = lax.dynamic_slice_in_dim(train, lax.axis_index("dp") * seqs, seqs, 0)
    n_col = 2 * n_pair
    rows = queries.shape[0] // n_col
    part = contract(train, queries).astype(jnp.bfloat16)
    part = part.reshape(n_dp * seqs, n_col, rows).transpose(1, 0, 2)
    scores = jnp.sum(exchange(part, COLS).astype(jnp.float32), axis=0).T
    return (sketches, scores)


def solution(mesh):
    n_dp, n_tensor = mesh.devices.shape
    fine = Mesh(mesh.devices.reshape(n_dp, n_tensor // 2, 2), ("dp",) + COLS)
    return jax.shard_map(
        per_device,
        mesh=fine,
        in_specs=(
            P("dp", COLS),
            P("dp", COLS),
            P("dp", COLS),
            P("dp", COLS),
            P(None, COLS),
            P(None, None, COLS),
            P("dp", COLS),
        ),
        out_specs=(P("dp", COLS), P(("dp",) + COLS, None)),
        check_vma=False,
    )
```

time: 474 us -> 101 us (0.21)
  the two profiles are of different devices: /device:TPU:2 before, /device:TPU:33 now
where the time goes in v1:
time: 101 us
  blocking collectives  64.3 us (64%)
  waiting for transfers between devices  24.3 us (24%)
  matrix products  4.29 us (4%)
  starting transfers between devices  3.97 us (4%)
  local copies, waits for them, and re-layouts  2.16 us (2%)
    all_to_all x2, blocking collectives, exchange(): lax.all_to_all(blocks, axes, split_axis=0, concat_axis=0, tiled=False)  64.3 us
    all_to_all x1, waiting for transfers between devices, exchange(): lax.all_to_all(blocks, axes, split_axis=0, concat_axis=0, tiled=False)  24.3 us
    dot_general x4, matrix products, contract(): lax.dot_general(left, right, (((1,), (1,)), ((), ())), preferred_element_...  4.13 us
    all_to_all x1, starting transfers between devices, exchange(): lax.all_to_all(blocks, axes, split_axis=0, concat_axis=0, tiled=False)  3.97 us
  transfers between devices with their start and end apart: 1, of which 1 were waited for; matrix products, arithmetic and copies ran while one was open for 1% of the time, Pallas kernels for 0%

profile of v1, /device:TPU:33, one launch (start us, length us, event | category | flops | bytes accessed | tf_op | source)
XLA Modules:
  0.0 100.5 jit_solution(12033911985414874617)
XLA Ops:
  0.6 0.0 copy-start
  0.6 0.0 copy-start.3
  0.7 0.0 copy-start.4
  0.7 2.9 %fusion.13 = f32[256,64]{0,1:T(8,128)S(1)} fusion(bf16[256,1792]{1,0:T(8,128)(2,1)} %param.10, bf16[256,1792]{1,0:T(8,128)(2,1)} %param.8, bf16[256,1792]{1,0:T(8,128)(2,1)} %param.9, bf16[2,64,1792]{2,1,0:T(8,128)(2,1)} %param.12), kind=kOutput, calls=%fused_computation.20 | convolution fusion | flops 64684032 | bytes 3047424 | tf_op jit(solution)/shard_map/dot_general | solution.py:11
  3.5 0.0 copy-done.3
  3.6 0.0 copy-start.1
  3.6 0.0 copy-start.2
  3.6 0.7 fusion.11
  4.2 0.3 copy-done.1
  4.5 0.2 convolution_convert_fusion.1
  4.8 44.1 %all_to_all.15 = bf16[16,40,256]{2,1,0:T(8,128)(2,1)S(1)} all-to-all(bf16[16,40,256]{2,1,0:T(8,128)(2,1)S(1)} %bitcast.40), channel_id=1, replica_groups=mesh['dp'=32,'pair'=8,'core'=2] {'pair','core'}, dimensions={0} | all-to-all | bytes 655360 | tf_op jit(solution)/shard_map/all_to_all | solution.py:17
  48.9 0.1 convert_reduce_fusion
  48.9 0.2 convolution_convert_fusion.2
  49.1 0.1 reshape.35
  49.2 20.3 %all_to_all.16 = bf16[64,2,128]{2,1,0:T(2,128)(2,1)S(1)} all-to-all(bf16[64,2,128]{2,1,0:T(2,128)(2,1)S(1)} %bitcast.42), channel_id=1, replica_groups=mesh['dp'=32,'pair'=8,'core'=2] {'dp','core'}, dimensions={0} | all-to-all | bytes 65536 | tf_op jit(solution)/shard_map/all_to_all | solution.py:17
  69.5 0.1 reshape.37
  69.6 0.1 copy.21
  69.7 0.1 reshape.38
  69.9 0.4 fusion.9
  70.3 0.8 copy.30
  71.1 4.0 %all-to-all-start.2 = ((bf16[16,64,128]{2,1,0:T(8,128)(2,1)}), bf16[16,64,128]{2,1,0:T(8,128)(2,1)S(1)}, u32[]{:S(2)}, u32[]{:S(2)}) async-start(bf16[16,64,128]{2,1,0:T(8,128)(2,1)} %bitcast.39), calls=%async_computation.2 | async-start | bytes 524288 | tf_op jit(solution)/shard_map/all_to_all | solution.py:17
  75.0 0.6 constant_dynamic-slice_fusion
  75.6 24.3 %all-to-all-done.2 = bf16[16,64,128]{2,1,0:T(8,128)(2,1)S(1)} async-done(((bf16[16,64,128]{2,1,0:T(8,128)(2,1)}), bf16[16,64,128]{2,1,0:T(8,128)(2,1)S(1)}, u32[]{:S(2)}, u32[]{:S(2)}) %all-to-all-start.2) | async-done | bytes 262176 | tf_op jit(solution)/shard_map/all_to_all | solution.py:17
  99.9 0.7 convert_reduce_fusion.1
  (11 shorter events, 0.1 us)
Async XLA Ops:
  0.6 69.2 %copy-start = (bf16[2048,256]{1,0:T(8,128)(2,1)S(1)}, bf16[2048,256]{1,0:T(8,128)(2,1)}, u32[]{:S(2)}) copy-start(bf16[2048,256]{1,0:T(8,128)(2,1)} %param.13) | copy-start | bytes 3145732
  0.6 2.9 %copy-start.3 = (bf16[256,1792]{1,0:T(8,128)(2,1)S(1)}, bf16[256,1792]{1,0:T(8,128)(2,1)}, u32[]{:S(2)}) copy-start(bf16[256,1792]{1,0:T(8,128)(2,1)} %param.10) | copy-start | bytes 2752516
  0.7 2.9 %copy-start.4 = (bf16[256,1792]{1,0:T(8,128)(2,1)S(1)}, bf16[256,1792]{1,0:T(8,128)(2,1)}, u32[]{:S(2)}) copy-start(bf16[256,1792]{1,0:T(8,128)(2,1)} %param.8) | copy-start | bytes 2752516
  0.7 2.9 %copy-start.5 = (bf16[2,64,1792]{2,1,0:T(8,128)(2,1)S(1)}, bf16[2,64,1792]{2,1,0:T(8,128)(2,1)}, u32[]{:S(2)}) copy-start(bf16[2,64,1792]{2,1,0:T(8,128)(2,1)} %param.12) | copy-start | bytes 1376260
  3.6 1.0 copy-start.1
  3.6 0.9 copy-start.2
  71.1 28.8 %all-to-all-start.2 = ((bf16[16,64,128]{2,1,0:T(8,128)(2,1)}), bf16[16,64,128]{2,1,0:T(8,128)(2,1)S(1)}, u32[]{:S(2)}, u32[]{:S(2)}) async-start(bf16[16,64,128]{2,1,0:T(8,128)(2,1)} %bitcast.39), calls=%async_computation.2 | async-start | bytes 524288 | tf_op jit(solution)/shard_map/all_to_all | solution.py:17

commit v2 on v1

v2 whole, which is shorter than its diff:
```python
import jax
import jax.numpy as jnp
from jax import lax
from jax.sharding import Mesh, PartitionSpec as P

SEQ_LEN = 128
COLS = ("x", "half", "core")
NEAR = ("x", "core")
SWAP = [(0, 1), (1, 0)]


def contract(left, right):
    return lax.dot_general(
        left, right, (((1,), (1,)), ((), ())), preferred_element_type=jnp.float32
    )


def exchange(blocks, axes):
    return lax.all_to_all(blocks, axes, split_axis=0, concat_axis=0, tiled=False)


def per_device(acts, gate_pre, up_pre, hidden_grad, proj_in, proj_out, queries):
    rank = proj_in.shape[0]
    tok = acts.shape[0]
    seqs = tok // SEQ_LEN
    n_dp, n_x = lax.axis_size("dp"), lax.axis_size("x")
    my_half = lax.axis_index("half")
    tall = rank // n_x
    wide = tall // 2
    half = rank // 2
    gate = gate_pre.astype(jnp.float32)
    upval = up_pre.astype(jnp.float32)
    grad = hidden_grad.astype(jnp.float32)
    sig = jax.nn.sigmoid(gate)
    gate_grad = (grad * upval * sig * (1.0 + gate * (1.0 - sig))).astype(jnp.bfloat16)
    up_grad = (grad * gate * sig).astype(jnp.bfloat16)
    out_t = contract(proj_out[0], gate_grad) + contract(proj_out[1], up_grad)
    in_t = contract(proj_in, acts)
    out_b = out_t.astype(jnp.bfloat16).reshape(n_x, 1, tall, tok)
    in_b = in_t.astype(jnp.bfloat16).reshape(1, 2, half, tok)
    parts = jnp.concatenate(
        [
            jnp.broadcast_to(out_b, (n_x, 2, tall, tok)),
            jnp.broadcast_to(in_b, (n_x, 2, half, tok)),
        ],
        axis=2,
    ).reshape(2 * n_x, tall + half, tok)
    near = jnp.sum(exchange(parts, NEAR).astype(jnp.float32), axis=0)
    far = lax.ppermute(near.astype(jnp.bfloat16), "half", SWAP)
    total = near + far.astype(jnp.float32)
    outs = lax.dynamic_slice_in_dim(total, my_half * wide, wide, 0)
    outs = outs.reshape(wide, seqs, SEQ_LEN)
    ins = total[tall:].reshape(half, seqs, SEQ_LEN)
    block = jnp.einsum("ast,bst->sab", outs, ins, precision=lax.Precision.HIGHEST)
    block = block.astype(jnp.bfloat16).reshape(seqs, 2, wide // 2 * half)
    sends = jnp.broadcast_to(block.transpose(1, 0, 2), (n_dp, 2, seqs, wide // 2 * half))
    sends = sends.reshape(n_dp * 2, seqs, wide // 2 * half)
    all_blocks = exchange(sends, ("dp", "core"))
    all_blocks = all_blocks.reshape(n_dp, 2, seqs, wide // 2, half)
    train = all_blocks.transpose(0, 2, 3, 1, 4).reshape(n_dp * seqs, wide // 2 * rank)
    sketches = lax.dynamic_slice_in_dim(train, lax.axis_index("dp") * seqs, seqs, 0)
    rows = queries.shape[0] // (4 * n_x)
    part = contract(train, queries).astype(jnp.bfloat16)
    part = part.reshape(n_dp * seqs, n_x, 2, 2, rows).transpose(1, 3, 2, 0, 4)
    part = part.reshape(2 * n_x, 2, n_dp * seqs, rows)
    near = jnp.sum(exchange(part, NEAR).astype(jnp.float32), axis=0)
    mine = lax.dynamic_index_in_dim(near, my_half, 0, keepdims=False)
    theirs = lax.dynamic_index_in_dim(near, 1 - my_half, 0, keepdims=False)
    far = lax.ppermute(theirs.astype(jnp.bfloat16), "half", SWAP)
    scores = (mine + far.astype(jnp.float32)).T
    return (sketches, scores)


def solution(mesh):
    n_dp, n_tensor = mesh.devices.shape
    fine = Mesh(mesh.devices.reshape(n_dp, n_tensor // 4, 2, 2), ("dp",) + COLS)
    return jax.shard_map(
        per_device,
        mesh=fine,
        in_specs=(
            P("dp", COLS),
            P("dp", COLS),
            P("dp", COLS),
            P("dp", COLS),
            P(None, COLS),
            P(None, None, COLS),
            P("dp", COLS),
        ),
        out_specs=(P("dp", COLS), P(("dp",) + COLS, None)),
        check_vma=False,
    )
```

time: 101 us -> 86.2 us (0.85)
  the two profiles are of different devices: /device:TPU:33 before, /device:TPU:1 now
where the time goes in v2:
time: 86.2 us; the launch traced here: 85.9 us
  blocking collectives  41.2 us (48%)
  starting transfers between devices  23.7 us (27%)
  waiting for transfers between devices  12.8 us (15%)
  matrix products  4.28 us (5%)
  local copies, waits for them, and re-layouts  2.35 us (3%)
    all_to_all x2, blocking collectives, exchange(): lax.all_to_all(blocks, axes, split_axis=0, concat_axis=0, tiled=False)  41.2 us
    ppermute x1, starting transfers between devices, per_device(): far = lax.ppermute(near.astype(jnp.bfloat16), 'half', SWAP)  11.8 us
    ppermute x1, starting transfers between devices, per_device(): far = lax.ppermute(theirs.astype(jnp.bfloat16), 'half', SWAP)  7.95 us
    all_to_all x1, waiting for transfers between devices, exchange(): lax.all_to_all(blocks, axes, split_axis=0, concat_axis=0, tiled=False)  6.52 us
    ppermute x1, waiting for transfers between devices, per_device(): far = lax.ppermute(theirs.astype(jnp.bfloat16), 'half', SWAP)  4.66 us
    dot_general x4, matrix products, contract(): lax.dot_general(left, right, (((1,), (1,)), ((), ())), preferred_element_...  4.14 us
    all_to_all x1, starting transfers between devices, exchange(): lax.all_to_all(blocks, axes, split_axis=0, concat_axis=0, tiled=False)  3.96 us
  transfers between devices with their start and end apart: 3, of which 3 were waited for; matrix products, arithmetic and copies ran while one was open for 1% of the time, Pallas kernels for 0%

profile of v2, /device:TPU:1, one launch (start us, length us, event | category | flops | bytes accessed | tf_op | source)
XLA Modules:
  0.0 85.9 jit_solution(5411073102579229890)
XLA Ops:
  0.6 0.0 copy-start
  0.7 2.9 %fusion.11 = f32[256,64]{0,1:T(8,128)S(1)} fusion(bf16[256,1792]{1,0:T(8,128)(2,1)} %param.10, bf16[256,1792]{1,0:T(8,128)(2,1)} %param.8, bf16[256,1792]{1,0:T(8,128)(2,1)} %param.9, bf16[2,64,1792]{2,1,0:T(8,128)(2,1)} %param.12), kind=kOutput, calls=%fused_computation.18 | convolution fusion | flops 64684032 | bytes 3047424 | tf_op jit(solution)/shard_map/dot_general | solution.py:13
  3.5 0.0 copy-done.3
  3.6 0.7 fusion.9
  4.2 0.3 copy-done.1
  4.5 0.2 convolution_convert_fusion.1
  4.8 15.2 %all_to_all.15 = bf16[8,48,256]{2,1,0:T(8,128)(2,1)S(1)} all-to-all(bf16[8,48,256]{2,1,0:T(8,128)(2,1)S(1)} %bitcast.41), channel_id=1, replica_groups=mesh['dp'=32,'x'=4,'half'=2,'core'=2] {'x','core'}, dimensions={0} | all-to-all | bytes 393216 | tf_op jit(solution)/shard_map/all_to_all | solution.py:19
  20.0 11.8 %collective-permute-start = (bf16[48,256]{1,0:T(8,128)(2,1)S(1)}, bf16[48,256]{1,0:T(8,128)(2,1)S(1)}, u32[]{:S(2)}, u32[]{:S(2)}) collective-permute-start(bf16[48,256]{1,0:T(8,128)(2,1)S(1)} %convert_element_type.60), channel_id=1, source_target_pairs={{0,2},{2,0},{1,3},{3,1},{4,6},{6,4},{5,7},{7,5},{8,10},{10,8},{9,1... | collective-permute-start | bytes 73736 | tf_op jit(solution)/shard_map/ppermute | solution.py:49
  31.8 1.6 %collective-permute-done = bf16[48,256]{1,0:T(8,128)(2,1)S(1)} collective-permute-done((bf16[48,256]{1,0:T(8,128)(2,1)S(1)}, bf16[48,256]{1,0:T(8,128)(2,1)S(1)}, u32[]{:S(2)}, u32[]{:S(2)}) %collective-permute-start) | collective-permute-done | bytes 24608 | tf_op jit(solution)/shard_map/ppermute | solution.py:49
  33.4 0.1 convolution_convert_fusion.2
  33.5 0.1 reshape.39
  33.7 26.1 %all_to_all.16 = bf16[64,2,128]{2,1,0:T(2,128)(2,1)S(1)} all-to-all(bf16[64,2,128]{2,1,0:T(2,128)(2,1)S(1)} %bitcast.43), channel_id=1, replica_groups=mesh['dp'=32,'x'=4,'half'=2,'core'=2] {'dp','core'}, dimensions={0} | all-to-all | bytes 65536 | tf_op jit(solution)/shard_map/all_to_all | solution.py:19
  59.8 0.1 reshape.41
  59.9 0.1 copy.23
  60.0 0.1 reshape.42
  60.1 0.4 convolution_convert_fusion
  60.6 0.2 reshape.43
  60.8 0.8 copy.24
  61.5 4.0 %all-to-all-start.2 = ((bf16[8,2,64,128]{3,2,1,0:T(8,128)(2,1)}), bf16[8,2,64,128]{3,2,1,0:T(8,128)(2,1)S(1)}, u32[]{:S(2)}, u32[]{:S(2)}) async-start(bf16[8,2,64,128]{3,2,1,0:T(8,128)(2,1)} %bitcast.11), calls=%async_computation.2 | async-start | bytes 524288 | tf_op jit(solution)/shard_map/all_to_all | solution.py:19
  65.5 6.5 %all-to-all-done.2 = bf16[8,2,64,128]{3,2,1,0:T(8,128)(2,1)S(1)} async-done(((bf16[8,2,64,128]{3,2,1,0:T(8,128)(2,1)}), bf16[8,2,64,128]{3,2,1,0:T(8,128)(2,1)S(1)}, u32[]{:S(2)}, u32[]{:S(2)}) %all-to-all-start.2) | async-done | bytes 262176 | tf_op jit(solution)/shard_map/all_to_all | solution.py:19
  72.1 7.9 %collective-permute-start.1 = (bf16[64,128]{1,0:T(8,128)(2,1)S(1)}, bf16[64,128]{1,0:T(8,128)(2,1)S(1)}, u32[]{:S(2)}, u32[]{:S(2)}) collective-permute-start(bf16[64,128]{1,0:T(8,128)(2,1)S(1)} %fusion.20), channel_id=1, source_target_pairs={{0,2},{2,0},{1,3},{3,1},{4,6},{6,4},{5,7},{7,5},{8,10},{10,8},{9,1... | collective-permute-start | bytes 49160 | tf_op jit(solution)/shard_map/ppermute | solution.py:69
  80.0 0.6 constant_dynamic-slice_fusion
  80.6 4.7 %collective-permute-done.1 = bf16[64,128]{1,0:T(8,128)(2,1)S(1)} collective-permute-done((bf16[64,128]{1,0:T(8,128)(2,1)S(1)}, bf16[64,128]{1,0:T(8,128)(2,1)S(1)}, u32[]{:S(2)}, u32[]{:S(2)}) %collective-permute-start.1) | collective-permute-done | bytes 16416 | tf_op jit(solution)/shard_map/ppermute | solution.py:69
  85.3 0.6 fusion.19
  (20 shorter events, 0.2 us)
Async XLA Ops:
  0.6 59.5 %copy-start = (bf16[2048,256]{1,0:T(8,128)(2,1)S(1)}, bf16[2048,256]{1,0:T(8,128)(2,1)}, u32[]{:S(2)}) copy-start(bf16[2048,256]{1,0:T(8,128)(2,1)} %param.13) | copy-start | bytes 3145732
  0.6 2.9 %copy-start.3 = (bf16[256,1792]{1,0:T(8,128)(2,1)S(1)}, bf16[256,1792]{1,0:T(8,128)(2,1)}, u32[]{:S(2)}) copy-start(bf16[256,1792]{1,0:T(8,128)(2,1)} %param.10) | copy-start | bytes 2752516
  0.7 2.9 %copy-start.4 = (bf16[256,1792]{1,0:T(8,128)(2,1)S(1)}, bf16[256,1792]{1,0:T(8,128)(2,1)}, u32[]{:S(2)}) copy-start(bf16[256,1792]{1,0:T(8,128)(2,1)} %param.8) | copy-start | bytes 2752516
  0.7 2.9 %copy-start.5 = (bf16[2,64,1792]{2,1,0:T(8,128)(2,1)S(1)}, bf16[2,64,1792]{2,1,0:T(8,128)(2,1)}, u32[]{:S(2)}) copy-start(bf16[2,64,1792]{2,1,0:T(8,128)(2,1)} %param.12) | copy-start | bytes 1376260
  3.6 1.0 %copy-start.1 = (bf16[256,512]{1,0:T(8,128)(2,1)S(1)}, bf16[256,512]{1,0:T(8,128)(2,1)}, u32[]{:S(2)}) copy-start(bf16[256,512]{1,0:T(8,128)(2,1)} %param.7) | copy-start | bytes 786436
  3.6 0.9 %copy-start.2 = (bf16[64,512]{1,0:T(8,128)(2,1)S(1)}, bf16[64,512]{1,0:T(8,128)(2,1)}, u32[]{:S(2)}) copy-start(bf16[64,512]{1,0:T(8,128)(2,1)} %param.11) | copy-start | bytes 196612
  20.0 13.4 %collective-permute-start = (bf16[48,256]{1,0:T(8,128)(2,1)S(1)}, bf16[48,256]{1,0:T(8,128)(2,1)S(1)}, u32[]{:S(2)}, u32[]{:S(2)}) collective-permute-start(bf16[48,256]{1,0:T(8,128)(2,1)S(1)} %convert_element_type.60), channel_id=1, source_target_pairs={{0,2},{2,0},{1,3},{3,1},{4,6},{6,4},{5,7},{7,5},{8,10},{10,8},{9,1... | collective-permute-start | bytes 73736 | tf_op jit(solution)/shard_map/ppermute | solution.py:49
  61.5 10.5 %all-to-all-start.2 = ((bf16[8,2,64,128]{3,2,1,0:T(8,128)(2,1)}), bf16[8,2,64,128]{3,2,1,0:T(8,128)(2,1)S(1)}, u32[]{:S(2)}, u32[]{:S(2)}) async-start(bf16[8,2,64,128]{3,2,1,0:T(8,128)(2,1)} %bitcast.11), calls=%async_computation.2 | async-start | bytes 524288 | tf_op jit(solution)/shard_map/all_to_all | solution.py:19
  72.1 13.2 %collective-permute-start.1 = (bf16[64,128]{1,0:T(8,128)(2,1)S(1)}, bf16[64,128]{1,0:T(8,128)(2,1)S(1)}, u32[]{:S(2)}, u32[]{:S(2)}) collective-permute-start(bf16[64,128]{1,0:T(8,128)(2,1)S(1)} %fusion.20), channel_id=1, source_target_pairs={{0,2},{2,0},{1,3},{3,1},{4,6},{6,4},{5,7},{7,5},{8,10},{10,8},{9,1... | collective-permute-start | bytes 49160 | tf_op jit(solution)/shard_map/ppermute | solution.py:69

commit v3 on v2

v3 whole, which is shorter than its diff:
```python
import functools

import jax
import jax.numpy as jnp
import numpy as np
from jax import lax
from jax.experimental import pallas as pl
from jax.experimental.pallas import tpu as pltpu
from jax.sharding import Mesh, PartitionSpec as P

SEQ_LEN = 128
COLS = ("x", "half", "core")
NEAR = ("x", "core")
SWAP = [(0, 1), (1, 0)]
VMEM = 16 * 1024 * 1024


def contract(left, right):
    return lax.dot_general(
        left, right, (((1,), (1,)), ((), ())), preferred_element_type=jnp.float32
    )


def exchange(blocks, axes):
    return lax.all_to_all(blocks, axes, split_axis=0, concat_axis=0, tiled=False)


def project_kernel(
    n_x, cuts, acts_hbm, gate_hbm, up_hbm, grad_hbm, pin_hbm, pout_hbm, parts,
    acts, gate_pre, up_pre, hidden_grad, proj_in, proj_out, gate_grad, up_grad, sems,
):
    def fetch(at, which, source, target):
        copy = pltpu.make_async_copy(source, target, sems.at[at, which])
        copy.start()
        return copy

    spans = [pl.ds(lo, hi - lo) for lo, hi in zip(cuts[:-1], cuts[1:], strict=True)]
    waits = []
    for at, span in enumerate(spans):
        waits.append(
            [
                fetch(at, 0, gate_hbm.at[:, span], gate_pre.at[:, span]),
                fetch(at, 1, grad_hbm.at[:, span], hidden_grad.at[:, span]),
                fetch(at, 2, up_hbm.at[:, span], up_pre.at[:, span]),
                fetch(at, 3, pout_hbm.at[:, :, span], proj_out.at[:, :, span]),
            ]
        )
    last = [
        fetch(len(spans), 0, acts_hbm, acts),
        fetch(len(spans), 1, pin_hbm, proj_in),
    ]
    tok = gate_pre.shape[0]
    total = None
    for at, (lo, hi) in enumerate(zip(cuts[:-1], cuts[1:], strict=True)):
        for copy in waits[at]:
            copy.wait()
        for col in range(lo, hi, 256):
            cols = slice(col, col + 256)
            for row in range(0, tok, 32):
                rows = slice(row, row + 32)
                gate = gate_pre[rows, cols].astype(jnp.float32)
                sig = 0.5 * jnp.tanh(0.5 * gate) + 0.5
                scaled = hidden_grad[rows, cols].astype(jnp.float32) * sig
                up_grad[rows, cols] = (scaled * gate).astype(jnp.bfloat16)
                slope = 1.0 + gate * (1.0 - sig)
                full = scaled * up_pre[rows, cols].astype(jnp.float32) * slope
                gate_grad[rows, cols] = full.astype(jnp.bfloat16)
            term = contract(proj_out[0, :, cols], gate_grad[:, cols])
            term += contract(proj_out[1, :, cols], up_grad[:, cols])
            total = term if total is None else total + term
    for copy in last:
        copy.wait()
    ins = contract(proj_in[...], acts[...]).astype(jnp.bfloat16)
    outs = total.astype(jnp.bfloat16)
    rank = outs.shape[0]
    tall, half = rank // n_x, rank // 2
    for x in range(n_x):
        for core in range(2):
            slot = 2 * x + core
            parts[slot, :tall] = outs[x * tall : (x + 1) * tall]
            parts[slot, tall:] = ins[core * half : (core + 1) * half]


def project(n_x, acts, gate_pre, up_pre, hidden_grad, proj_in, proj_out):
    tok, hidden = gate_pre.shape
    rank = proj_in.shape[0]
    cuts = (0,) + tuple(range(256, hidden + 1, 512))
    shape = (2 * n_x, rank // n_x + rank // 2, tok)
    given = (acts, gate_pre, up_pre, hidden_grad, proj_in, proj_out)
    held = [pltpu.VMEM(a.shape, a.dtype) for a in given]
    grads = [pltpu.VMEM((tok, hidden), jnp.bfloat16)] * 2
    return pl.pallas_call(
        functools.partial(project_kernel, n_x, cuts),
        in_specs=[pl.BlockSpec(memory_space=pltpu.HBM)] * len(given),
        out_specs=pl.BlockSpec(memory_space=pltpu.VMEM),
        out_shape=pltpu.VMEM(shape, jnp.bfloat16),
        scratch_shapes=held + grads + [pltpu.SemaphoreType.DMA((len(cuts), 4))],
        compiler_params=pltpu.CompilerParams(vmem_limit_bytes=VMEM),
    )(*[pltpu.with_memory_space_constraint(a, pltpu.HBM) for a in given])


def score_kernel(n_x, blocks, place, queries, part):
    one = jnp.dot(blocks[0], place[0], preferred_element_type=jnp.float32)
    two = jnp.dot(blocks[1], place[1], preferred_element_type=jnp.float32)
    train = (one + two).astype(jnp.bfloat16)
    rows = part.shape[3]
    for x in range(n_x):
        for half in range(2):
            at = (4 * x + 2 * half) * rows
            both = contract(train, queries[at : at + 2 * rows]).astype(jnp.bfloat16)
            part[2 * x, half] = both[:, :rows]
            part[2 * x + 1, half] = both[:, rows:]


def partial_scores(n_x, blocks, place, queries):
    n_seq = blocks.shape[1]
    rows = queries.shape[0] // (4 * n_x)
    vmem = pl.BlockSpec(memory_space=pltpu.VMEM)
    return pl.pallas_call(
        functools.partial(score_kernel, n_x),
        in_specs=[vmem, vmem, vmem],
        out_specs=vmem,
        out_shape=pltpu.VMEM((2 * n_x, 2, n_seq, rows), jnp.bfloat16),
        compiler_params=pltpu.CompilerParams(vmem_limit_bytes=VMEM),
    )(blocks, place, queries)


def per_device(acts, gate_pre, up_pre, hidden_grad, proj_in, proj_out, queries):
    rank = proj_in.shape[0]
    tok = acts.shape[0]
    seqs = tok // SEQ_LEN
    n_dp, n_x = lax.axis_size("dp"), lax.axis_size("x")
    my_half = lax.axis_index("half")
    tall = rank // n_x
    wide = tall // 2
    few = wide // 2
    half = rank // 2
    parts = project(n_x, acts, gate_pre, up_pre, hidden_grad, proj_in, proj_out)
    near = jnp.sum(exchange(parts, NEAR).astype(jnp.float32), axis=0)
    far = lax.ppermute(near.astype(jnp.bfloat16), "half", SWAP)
    total = near + far.astype(jnp.float32)
    outs = lax.dynamic_slice_in_dim(total, my_half * wide, wide, 0)
    outs = outs.reshape(wide, seqs, SEQ_LEN)
    ins = total[tall:].reshape(half, seqs, SEQ_LEN)
    block = jnp.einsum("ast,bst->sab", outs, ins, precision=lax.Precision.HIGHEST)
    block = block.astype(jnp.bfloat16).reshape(seqs, 2, few * half)
    sends = jnp.broadcast_to(block.transpose(1, 0, 2)[:, None], (2, n_dp, seqs, few * half))
    sends = sends.reshape(n_dp * 2, seqs, few * half)
    got = exchange(sends, ("core", "dp")).reshape(2, n_dp * seqs, few * half)
    src = np.arange(few * half)[:, None]
    dst = src // half * rank + src % half
    col = np.arange(few * rank)[None, :]
    place = np.stack([col == dst, col == dst + half]).astype(jnp.bfloat16)
    part = partial_scores(n_x, got, place, queries)
    near = jnp.sum(exchange(part, NEAR).astype(jnp.float32), axis=0)
    near, got = lax.optimization_barrier((near, got))
    own = lax.dynamic_slice_in_dim(got, lax.axis_index("dp") * seqs, seqs, 1)
    own = own.reshape(2, seqs, few, half).transpose(1, 2, 0, 3)
    sketches = own.reshape(seqs, few * rank)
    mine = lax.dynamic_index_in_dim(near, my_half, 0, keepdims=False)
    theirs = lax.dynamic_index_in_dim(near, 1 - my_half, 0, keepdims=False)
    far = lax.ppermute(theirs.astype(jnp.bfloat16), "half", SWAP)
    scores = (mine + far.astype(jnp.float32)).T
    return (sketches, scores)


def solution(mesh):
    n_dp, n_tensor = mesh.devices.shape
    fine = Mesh(mesh.devices.reshape(n_dp, n_tensor // 4, 2, 2), ("dp",) + COLS)
    return jax.shard_map(
        per_device,
        mesh=fine,
        in_specs=(
            P("dp", COLS),
            P("dp", COLS),
            P("dp", COLS),
            P("dp", COLS),
            P(None, COLS),
            P(None, None, COLS),
            P("dp", COLS),
        ),
        out_specs=(P("dp", COLS), P(("dp",) + COLS, None)),
        check_vma=False,
    )
```

time: 86.2 us -> 84.4 us (0.979)
  Pallas kernels: 0 us -> 4.33 us
  matrix products: 4.28 us -> 0.15 us
  local copies, waits for them, and re-layouts: 2.35 us -> 0.92 us
    pallas_call x0 -> x2, Pallas kernels: none -> 4.33 us  [the longest x1 3.12 us: project(): pl.pallas_call(functools.partial(project_kernel, n_x, cuts), in_specs=[pl...]
    dot_general x4 -> x0, matrix products: 4.14 us -> none  [contract(): lax.dot_general(left, right, (((1,), (1,)), ((), ())), preferred_element_...]
where the time goes in v3:
time: 84.4 us; the launch traced here: 84.1 us
  blocking collectives  40.8 us (48%)
  starting transfers between devices  23.9 us (28%)
  waiting for transfers between devices  12.6 us (15%)
  Pallas kernels  4.33 us (5%)
  local copies, waits for them, and re-layouts  0.92 us (1%)
    all_to_all x2, blocking collectives, exchange(): lax.all_to_all(blocks, axes, split_axis=0, concat_axis=0, tiled=False)  40.8 us
    ppermute x1, starting transfers between devices, per_device(): far = lax.ppermute(near.astype(jnp.bfloat16), 'half', SWAP)  11.8 us
    ppermute x1, starting transfers between devices, per_device(): far = lax.ppermute(theirs.astype(jnp.bfloat16), 'half', SWAP)  7.94 us
    all_to_all x1, waiting for transfers between devices, exchange(): lax.all_to_all(blocks, axes, split_axis=0, concat_axis=0, tiled=False)  6.52 us
    ppermute x1, waiting for transfers between devices, per_device(): far = lax.ppermute(theirs.astype(jnp.bfloat16), 'half', SWAP)  4.48 us
    all_to_all x1, starting transfers between devices, exchange(): lax.all_to_all(blocks, axes, split_axis=0, concat_axis=0, tiled=False)  4.17 us
    pallas_call x1, Pallas kernels, project(): pl.pallas_call(functools.partial(project_kernel, n_x, cuts), in_specs=[pl...  3.12 us
  transfers between devices with their start and end apart: 3, of which 3 were waited for; matrix products, arithmetic and copies ran while one was open for 1% of the time, Pallas kernels for 0%

profile of v3, /device:TPU:1, one launch (start us, length us, event | category | flops | bytes accessed | tf_op | source)
XLA Modules:
  0.0 84.1 jit_solution(10648119628298038724)
XLA Ops:
  0.6 0.0 copy-start
  0.6 3.1 %shard_map.95 = bf16[8,48,256]{2,1,0:T(8,128)(2,1)S(1)} custom-call(bf16[256,512]{1,0:T(8,128)(2,1)} %acts_hbm.1, bf16[256,1792]{1,0:T(8,128)(2,1)} %gate_hbm.1, bf16[256,1792]{1,0:T(8,128)(2,1)} %up_hbm.1, bf16[256,1792]{1,0:T(8,128)(2,1)} %grad_hbm.1, bf16[64,512]{1,0:T(8,128)(2,1)} %pin_hbm.1, bf16[2,64,1792]{2,1,0:T(8,128)(2,1)} %pout_hbm.1), custom_call_target="tpu_custom_call" | custom-call | tf_op jit(solution)/shard_map/pallas_call | solution.py:92
  3.8 15.2 %all_to_all.15 = bf16[8,48,256]{2,1,0:T(8,128)(2,1)S(1)} all-to-all(bf16[8,48,256]{2,1,0:T(8,128)(2,1)S(1)} %shard_map.95), channel_id=1, replica_groups=mesh['dp'=32,'x'=4,'half'=2,'core'=2] {'x','core'}, dimensions={0} | all-to-all | bytes 393216 | tf_op jit(solution)/shard_map/all_to_all | solution.py:25
  19.0 11.8 %collective-permute-start = (bf16[48,256]{1,0:T(8,128)(2,1)S(1)}, bf16[48,256]{1,0:T(8,128)(2,1)S(1)}, u32[]{:S(2)}, u32[]{:S(2)}) collective-permute-start(bf16[48,256]{1,0:T(8,128)(2,1)S(1)} %convert_element_type.25), channel_id=1, source_target_pairs={{0,2},{2,0},{1,3},{3,1},{4,6},{6,4},{5,7},{7,5},{8,10},{10,8},{9,1... | collective-permute-start | bytes 73736 | tf_op jit(solution)/shard_map/ppermute | solution.py:140
  30.8 0.0 copy-start.1
  30.8 1.6 %collective-permute-done = bf16[48,256]{1,0:T(8,128)(2,1)S(1)} collective-permute-done((bf16[48,256]{1,0:T(8,128)(2,1)S(1)}, bf16[48,256]{1,0:T(8,128)(2,1)S(1)}, u32[]{:S(2)}, u32[]{:S(2)}) %collective-permute-start) | collective-permute-done | bytes 24608 | tf_op jit(solution)/shard_map/ppermute | solution.py:140
  32.4 0.1 convolution_convert_fusion
  32.5 0.1 reshape.29
  32.7 25.6 %all_to_all.16 = bf16[64,2,128]{2,1,0:T(2,128)(2,1)S(1)} all-to-all(bf16[64,2,128]{2,1,0:T(2,128)(2,1)S(1)} %bitcast.24), channel_id=1, replica_groups=mesh['dp'=32,'x'=4,'half'=2,'core'=2] {'core','dp'}, dimensions={0} | all-to-all | bytes 65536 | tf_op jit(solution)/shard_map/all_to_all | solution.py:25
  58.3 0.0 copy-done
  58.3 0.0 copy-done.1
  58.3 1.2 %shard_map.96 = bf16[8,2,64,128]{3,2,1,0:T(8,128)(2,1)} custom-call(bf16[2,64,128]{2,1,0:T(8,128)(2,1)S(1)} %bitcast.22, bf16[2,128,256]{2,1,0:T(8,128)(2,1)S(1)} %copy-done.1, bf16[2048,256]{1,0:T(8,128)(2,1)S(1)} %copy-done), custom_call_target="tpu_custom_call" | custom-call | tf_op jit(solution)/shard_map/pallas_call | solution.py:119
  59.5 4.2 %all-to-all-start.2 = ((bf16[8,2,64,128]{3,2,1,0:T(8,128)(2,1)}), bf16[8,2,64,128]{3,2,1,0:T(8,128)(2,1)S(1)}, u32[]{:S(2)}, u32[]{:S(2)}) async-start(bf16[8,2,64,128]{3,2,1,0:T(8,128)(2,1)} %shard_map.96), calls=%async_computation.2 | async-start | bytes 524288 | tf_op jit(solution)/shard_map/all_to_all | solution.py:25
  63.7 6.5 %all-to-all-done.2 = bf16[8,2,64,128]{3,2,1,0:T(8,128)(2,1)S(1)} async-done(((bf16[8,2,64,128]{3,2,1,0:T(8,128)(2,1)}), bf16[8,2,64,128]{3,2,1,0:T(8,128)(2,1)S(1)}, u32[]{:S(2)}, u32[]{:S(2)}) %all-to-all-start.2) | async-done | bytes 262176 | tf_op jit(solution)/shard_map/all_to_all | solution.py:25
  70.3 7.9 %collective-permute-start.1 = (bf16[64,128]{1,0:T(8,128)(2,1)S(1)}, bf16[64,128]{1,0:T(8,128)(2,1)S(1)}, u32[]{:S(2)}, u32[]{:S(2)}) collective-permute-start(bf16[64,128]{1,0:T(8,128)(2,1)S(1)} %fusion.3), channel_id=1, source_target_pairs={{0,2},{2,0},{1,3},{3,1},{4,6},{6,4},{5,7},{7,5},{8,10},{10,8},{9,1... | collective-permute-start | bytes 49160 | tf_op jit(solution)/shard_map/ppermute | solution.py:162
  78.2 0.1 reshape.32
  78.3 0.7 reshape.33
  79.0 4.5 %collective-permute-done.1 = bf16[64,128]{1,0:T(8,128)(2,1)S(1)} collective-permute-done((bf16[64,128]{1,0:T(8,128)(2,1)S(1)}, bf16[64,128]{1,0:T(8,128)(2,1)S(1)}, u32[]{:S(2)}, u32[]{:S(2)}) %collective-permute-start.1) | collective-permute-done | bytes 16416 | tf_op jit(solution)/shard_map/ppermute | solution.py:162
  83.5 0.6 fusion.2
  (9 shorter events, 0.2 us)
Async XLA Ops:
  0.6 57.7 %copy-start = (bf16[2048,256]{1,0:T(8,128)(2,1)S(1)}, bf16[2048,256]{1,0:T(8,128)(2,1)}, u32[]{:S(2)}) copy-start(bf16[2048,256]{1,0:T(8,128)(2,1)} %queries.1) | copy-start | bytes 3145732
  19.0 13.4 %collective-permute-start = (bf16[48,256]{1,0:T(8,128)(2,1)S(1)}, bf16[48,256]{1,0:T(8,128)(2,1)S(1)}, u32[]{:S(2)}, u32[]{:S(2)}) collective-permute-start(bf16[48,256]{1,0:T(8,128)(2,1)S(1)} %convert_element_type.25), channel_id=1, source_target_pairs={{0,2},{2,0},{1,3},{3,1},{4,6},{6,4},{5,7},{7,5},{8,10},{10,8},{9,1... | collective-permute-start | bytes 73736 | tf_op jit(solution)/shard_map/ppermute | solution.py:140
  30.8 27.5 %copy-start.1 = (bf16[2,128,256]{2,1,0:T(8,128)(2,1)S(1)}, bf16[2,128,256]{2,1,0:T(8,128)(2,1)}, u32[]{:S(2)}) copy-start(bf16[2,128,256]{2,1,0:T(8,128)(2,1)} %constant.34.clone.place) | copy-start | bytes 393220
  59.5 10.7 %all-to-all-start.2 = ((bf16[8,2,64,128]{3,2,1,0:T(8,128)(2,1)}), bf16[8,2,64,128]{3,2,1,0:T(8,128)(2,1)S(1)}, u32[]{:S(2)}, u32[]{:S(2)}) async-start(bf16[8,2,64,128]{3,2,1,0:T(8,128)(2,1)} %shard_map.96), calls=%async_computation.2 | async-start | bytes 524288 | tf_op jit(solution)/shard_map/all_to_all | solution.py:25
  70.3 13.2 %collective-permute-start.1 = (bf16[64,128]{1,0:T(8,128)(2,1)S(1)}, bf16[64,128]{1,0:T(8,128)(2,1)S(1)}, u32[]{:S(2)}, u32[]{:S(2)}) collective-permute-start(bf16[64,128]{1,0:T(8,128)(2,1)S(1)} %fusion.3), channel_id=1, source_target_pairs={{0,2},{2,0},{1,3},{3,1},{4,6},{6,4},{5,7},{7,5},{8,10},{10,8},{9,1... | collective-permute-start | bytes 49160 | tf_op jit(solution)/shard_map/ppermute | solution.py:162

commit v4 on v3

--- a/solution.py
+++ b/solution.py
@@ -10,7 +10,6 @@
 
 SEQ_LEN = 128
 COLS = ("x", "half", "core")
-NEAR = ("x", "core")
 SWAP = [(0, 1), (1, 0)]
 VMEM = 16 * 1024 * 1024
 
@@ -76,7 +75,7 @@
     tall, half = rank // n_x, rank // 2
     for x in range(n_x):
         for core in range(2):
-            slot = 2 * x + core
+            slot = core * n_x + x
             parts[slot, :tall] = outs[x * tall : (x + 1) * tall]
             parts[slot, tall:] = ins[core * half : (core + 1) * half]
 
@@ -108,8 +107,8 @@
         for half in range(2):
             at = (4 * x + 2 * half) * rows
             both = contract(train, queries[at : at + 2 * rows]).astype(jnp.bfloat16)
-            part[2 * x, half] = both[:, :rows]
-            part[2 * x + 1, half] = both[:, rows:]
+            part[x, half] = both[:, :rows]
+            part[n_x + x, half] = both[:, rows:]
 
 
 def partial_scores(n_x, blocks, place, queries):
@@ -123,6 +122,59 @@
         out_shape=pltpu.VMEM((2 * n_x, 2, n_seq, rows), jnp.bfloat16),
         compiler_params=pltpu.CompilerParams(vmem_limit_bytes=VMEM),
     )(blocks, place, queries)
+
+
+def own_kernel(seqs, blocks, place, sketches):
+    n_seq = blocks.shape[1]
+    row = lax.broadcasted_iota(jnp.int32, (8, n_seq), 0)
+    seq = lax.broadcasted_iota(jnp.int32, (8, n_seq), 1)
+    pick = (seq == lax.axis_index("dp") * seqs + row).astype(jnp.bfloat16)
+    total = None
+    for side in range(2):
+        lines = jnp.dot(pick, blocks[side], preferred_element_type=jnp.float32)
+        lines = lines.astype(jnp.bfloat16)
+        term = jnp.dot(lines, place[side], preferred_element_type=jnp.float32)
+        total = term if total is None else total + term
+    sketches[...] = total[:seqs].astype(jnp.bfloat16)
+
+
+def own_sketches(seqs, blocks, place):
+    vmem = pl.BlockSpec(memory_space=pltpu.VMEM)
+    return pl.pallas_call(
+        functools.partial(own_kernel, seqs),
+        in_specs=[vmem, vmem],
+        out_specs=vmem,
+        out_shape=jax.ShapeDtypeStruct((seqs, place.shape[2]), jnp.bfloat16),
+        compiler_params=pltpu.CompilerParams(vmem_limit_bytes=VMEM),
+    )(blocks, place)
+
+
+def split_kernel(got, mine, theirs):
+    half = lax.axis_index("half")
+
+    def add(which):
+        total = got[0, which].astype(jnp.float32)
+        for x in range(1, got.shape[0]):
+            total += got[x, which].astype(jnp.float32)
+        return total
+
+    mine[...] = add(half)
+    theirs[...] = add(1 - half).astype(jnp.bfloat16)
+
+
+def split_scores(got):
+    shape = got.shape[2:]
+    vmem = pl.BlockSpec(memory_space=pltpu.VMEM)
+    return pl.pallas_call(
+        split_kernel,
+        in_specs=[vmem],
+        out_specs=[vmem, vmem],
+        out_shape=[
+            pltpu.VMEM(shape, jnp.float32),
+            jax.ShapeDtypeStruct(shape, jnp.bfloat16),
+        ],
+        compiler_params=pltpu.CompilerParams(vmem_limit_bytes=VMEM),
+    )(got)
 
 
 def per_device(acts, gate_pre, up_pre, hidden_grad, proj_in, proj_out, queries):
@@ -130,36 +182,31 @@
     tok = acts.shape[0]
     seqs = tok // SEQ_LEN
     n_dp, n_x = lax.axis_size("dp"), lax.axis_size("x")
-    my_half = lax.axis_index("half")
     tall = rank // n_x
     wide = tall // 2
     few = wide // 2
     half = rank // 2
     parts = project(n_x, acts, gate_pre, up_pre, hidden_grad, proj_in, proj_out)
-    near = jnp.sum(exchange(parts, NEAR).astype(jnp.float32), axis=0)
+    near = jnp.sum(exchange(parts, ("core", "x")).astype(jnp.float32), axis=0)
     far = lax.ppermute(near.astype(jnp.bfloat16), "half", SWAP)
     total = near + far.astype(jnp.float32)
-    outs = lax.dynamic_slice_in_dim(total, my_half * wide, wide, 0)
+    outs = lax.dynamic_slice_in_dim(total, lax.axis_index("half") * wide, wide, 0)
     outs = outs.reshape(wide, seqs, SEQ_LEN)
     ins = total[tall:].reshape(half, seqs, SEQ_LEN)
     block = jnp.einsum("ast,bst->sab", outs, ins, precision=lax.Precision.HIGHEST)
     block = block.astype(jnp.bfloat16).reshape(seqs, 2, few * half)
     sends = jnp.broadcast_to(block.transpose(1, 0, 2)[:, None], (2, n_dp, seqs, few * half))
-    sends = sends.reshape(n_dp * 2, seqs, few * half)
+    sends = sends.reshape(2 * n_dp, seqs, few * half)
     got = exchange(sends, ("core", "dp")).reshape(2, n_dp * seqs, few * half)
     src = np.arange(few * half)[:, None]
     dst = src // half * rank + src % half
     col = np.arange(few * rank)[None, :]
     place = np.stack([col == dst, col == dst + half]).astype(jnp.bfloat16)
     part = partial_scores(n_x, got, place, queries)
-    near = jnp.sum(exchange(part, NEAR).astype(jnp.float32), axis=0)
-    near, got = lax.optimization_barrier((near, got))
-    own = lax.dynamic_slice_in_dim(got, lax.axis_index("dp") * seqs, seqs, 1)
-    own = own.reshape(2, seqs, few, half).transpose(1, 2, 0, 3)
-    sketches = own.reshape(seqs, few * rank)
-    mine = lax.dynamic_index_in_dim(near, my_half, 0, keepdims=False)
-    theirs = lax.dynamic_index_in_dim(near, 1 - my_half, 0, keepdims=False)
-    far = lax.ppermute(theirs.astype(jnp.bfloat16), "half", SWAP)
+    mine, theirs = split_scores(exchange(part, ("core", "x")))
+    theirs, got = lax.optimization_barrier((theirs, got))
+    far = lax.ppermute(theirs, "half", SWAP)
+    sketches = own_sketches(seqs, got, place)
     scores = (mine + far.astype(jnp.float32)).T
     return (sketches, scores)
 

time: 84.4 us -> 82.6 us (0.979)
  blocking collectives: 40.8 us -> 50.5 us
  waiting for transfers between devices: 12.6 us -> 5.92 us
  starting transfers between devices: 23.9 us -> 19.7 us
    all_to_all x2 -> x3, blocking collectives: 40.8 us -> 50.5 us  [exchange(): lax.all_to_all(blocks, axes, split_axis=0, concat_axis=0, tiled=False)]
    all_to_all x1 -> x0, waiting for transfers between devices: 6.52 us -> none  [exchange(): lax.all_to_all(blocks, axes, split_axis=0, concat_axis=0, tiled=False)]
    all_to_all x1 -> x0, starting transfers between devices: 4.17 us -> none  [exchange(): lax.all_to_all(blocks, axes, split_axis=0, concat_axis=0, tiled=False)]
    pallas_call x0 -> x2, Pallas kernels: none -> 0.85 us  [the longest x1 0.81 us: own_sketches(): pl.pallas_call(functools.partial(own_kernel, seqs), in_specs=[vmem, vmem]...]
  transfers between devices with their start and end apart: 3 -> 2, of which waited for: 3 -> 2; matrix products, arithmetic and copies ran while one was open for 1% -> 0% of each run, Pallas kernels for 0% -> 1%
where the time goes in v4:
time: 82.6 us; the launch traced here: 82.3 us
  blocking collectives  50.5 us (61%)
  starting transfers between devices  19.7 us (24%)
  waiting for transfers between devices  5.92 us (7%)
  Pallas kernels  4.47 us (5%)
    all_to_all x3, blocking collectives, exchange(): lax.all_to_all(blocks, axes, split_axis=0, concat_axis=0, tiled=False)  50.5 us
    ppermute x1, starting transfers between devices, per_device(): far = lax.ppermute(near.astype(jnp.bfloat16), 'half', SWAP)  11.8 us
    ppermute x1, starting transfers between devices, per_device(): far = lax.ppermute(theirs, 'half', SWAP)  7.95 us
    ppermute x1, waiting for transfers between devices, per_device(): far = lax.ppermute(theirs, 'half', SWAP)  4.43 us
    pallas_call x1, Pallas kernels, project(): pl.pallas_call(functools.partial(project_kernel, n_x, cuts), in_specs=[pl...  3.12 us
  transfers between devices with their start and end apart: 2, of which 2 were waited for; matrix products, arithmetic and copies ran while one was open for 0% of the time, Pallas kernels for 1%

profile of v4, /device:TPU:1, one launch (start us, length us, event | category | flops | bytes accessed | tf_op | source)
XLA Modules:
  0.0 82.3 jit_solution(15240472059544118031)
XLA Ops:
  0.6 0.0 copy-start
  0.6 3.1 %shard_map.95 = bf16[8,48,256]{2,1,0:T(8,128)(2,1)S(1)} custom-call(bf16[256,512]{1,0:T(8,128)(2,1)} %acts_hbm.1, bf16[256,1792]{1,0:T(8,128)(2,1)} %gate_hbm.1, bf16[256,1792]{1,0:T(8,128)(2,1)} %up_hbm.1, bf16[256,1792]{1,0:T(8,128)(2,1)} %grad_hbm.1, bf16[64,512]{1,0:T(8,128)(2,1)} %pin_hbm.1, bf16[2,64,1792]{2,1,0:T(8,128)(2,1)} %pout_hbm.1), custom_call_target="tpu_custom_call" | custom-call | tf_op jit(solution)/shard_map/pallas_call | solution.py:91
  3.8 15.2 %all_to_all.15 = bf16[8,48,256]{2,1,0:T(8,128)(2,1)S(1)} all-to-all(bf16[8,48,256]{2,1,0:T(8,128)(2,1)S(1)} %shard_map.95), channel_id=1, replica_groups=mesh['dp'=32,'x'=4,'half'=2,'core'=2] {'core','x'}, dimensions={0} | all-to-all | bytes 393216 | tf_op jit(solution)/shard_map/all_to_all | solution.py:24
  19.0 11.8 %collective-permute-start = (bf16[48,256]{1,0:T(8,128)(2,1)S(1)}, bf16[48,256]{1,0:T(8,128)(2,1)S(1)}, u32[]{:S(2)}, u32[]{:S(2)}) collective-permute-start(bf16[48,256]{1,0:T(8,128)(2,1)S(1)} %convert_element_type.16), channel_id=1, source_target_pairs={{0,2},{2,0},{1,3},{3,1},{4,6},{6,4},{5,7},{7,5},{8,10},{10,8},{9,1... | collective-permute-start | bytes 73736 | tf_op jit(solution)/shard_map/ppermute | solution.py:191
  30.8 0.0 copy-start.1
  30.8 1.5 %collective-permute-done = bf16[48,256]{1,0:T(8,128)(2,1)S(1)} collective-permute-done((bf16[48,256]{1,0:T(8,128)(2,1)S(1)}, bf16[48,256]{1,0:T(8,128)(2,1)S(1)}, u32[]{:S(2)}, u32[]{:S(2)}) %collective-permute-start) | collective-permute-done | bytes 24608 | tf_op jit(solution)/shard_map/ppermute | solution.py:191
  32.3 0.1 convolution_convert_fusion
  32.4 0.1 reshape.22
  32.6 25.2 %all_to_all.16 = bf16[64,2,128]{2,1,0:T(2,128)(2,1)S(1)} all-to-all(bf16[64,2,128]{2,1,0:T(2,128)(2,1)S(1)} %bitcast.17), channel_id=1, replica_groups=mesh['dp'=32,'x'=4,'half'=2,'core'=2] {'core','dp'}, dimensions={0} | all-to-all | bytes 65536 | tf_op jit(solution)/shard_map/all_to_all | solution.py:24
  57.7 0.0 copy-done
  57.7 0.0 copy-done.1
  57.7 0.5 shard_map.96
  58.3 10.2 %all_to_all.17.got = bf16[8,2,64,128]{3,2,1,0:T(8,128)(2,1)S(1)} all-to-all(bf16[8,2,64,128]{3,2,1,0:T(8,128)(2,1)S(1)} %shard_map.96), channel_id=1, replica_groups=mesh['dp'=32,'x'=4,'half'=2,'core'=2] {'core','x'}, dimensions={0} | all-to-all | bytes 524288 | tf_op jit(solution)/shard_map/all_to_all | solution.py:24
  68.5 7.9 %collective-permute-start.1 = (bf16[64,128]{1,0:T(8,128)(2,1)S(1)}, bf16[64,128]{1,0:T(8,128)(2,1)S(1)}, u32[]{:S(2)}, u32[]{:S(2)}) collective-permute-start(bf16[64,128]{1,0:T(8,128)(2,1)S(1)} %get-tuple-element.9), channel_id=1, source_target_pairs={{0,2},{2,0},{1,3},{3,1},{4,6},{6,4},{5,7},{7,5},{8,10},{10,8},{9,1... | collective-permute-start | bytes 49160 | tf_op jit(solution)/shard_map/ppermute | solution.py:208
  76.5 0.8 shard_map.98
  77.3 4.4 %collective-permute-done.1 = bf16[64,128]{1,0:T(8,128)(2,1)S(1)} collective-permute-done((bf16[64,128]{1,0:T(8,128)(2,1)S(1)}, bf16[64,128]{1,0:T(8,128)(2,1)S(1)}, u32[]{:S(2)}, u32[]{:S(2)}) %collective-permute-start.1) | collective-permute-done | bytes 16416 | tf_op jit(solution)/shard_map/ppermute | solution.py:208
  81.7 0.6 add_bitcast_fusion
  (6 shorter events, 0.1 us)
Async XLA Ops:
  0.6 57.1 %copy-start = (bf16[2048,256]{1,0:T(8,128)(2,1)S(1)}, bf16[2048,256]{1,0:T(8,128)(2,1)}, u32[]{:S(2)}) copy-start(bf16[2048,256]{1,0:T(8,128)(2,1)} %queries.1) | copy-start | bytes 3145732
  19.0 13.3 %collective-permute-start = (bf16[48,256]{1,0:T(8,128)(2,1)S(1)}, bf16[48,256]{1,0:T(8,128)(2,1)S(1)}, u32[]{:S(2)}, u32[]{:S(2)}) collective-permute-start(bf16[48,256]{1,0:T(8,128)(2,1)S(1)} %convert_element_type.16), channel_id=1, source_target_pairs={{0,2},{2,0},{1,3},{3,1},{4,6},{6,4},{5,7},{7,5},{8,10},{10,8},{9,1... | collective-permute-start | bytes 73736 | tf_op jit(solution)/shard_map/ppermute | solution.py:191
  30.8 27.0 %copy-start.1 = (bf16[2,128,256]{2,1,0:T(8,128)(2,1)S(1)}, bf16[2,128,256]{2,1,0:T(8,128)(2,1)}, u32[]{:S(2)}) copy-start(bf16[2,128,256]{2,1,0:T(8,128)(2,1)} %constant.14.clone.place) | copy-start | bytes 393220
  68.5 13.2 %collective-permute-start.1 = (bf16[64,128]{1,0:T(8,128)(2,1)S(1)}, bf16[64,128]{1,0:T(8,128)(2,1)S(1)}, u32[]{:S(2)}, u32[]{:S(2)}) collective-permute-start(bf16[64,128]{1,0:T(8,128)(2,1)S(1)} %get-tuple-element.9), channel_id=1, source_target_pairs={{0,2},{2,0},{1,3},{3,1},{4,6},{6,4},{5,7},{7,5},{8,10},{10,8},{9,1... | collective-permute-start | bytes 49160 | tf_op jit(solution)/shard_map/ppermute | solution.py:208

commit v5 on v4

--- a/solution.py
+++ b/solution.py
@@ -9,6 +9,7 @@
 from jax.sharding import Mesh, PartitionSpec as P
 
 SEQ_LEN = 128
+DP = ("y", "low")
 COLS = ("x", "half", "core")
 SWAP = [(0, 1), (1, 0)]
 VMEM = 16 * 1024 * 1024
@@ -26,7 +27,7 @@
 
 def project_kernel(
     n_x, cuts, acts_hbm, gate_hbm, up_hbm, grad_hbm, pin_hbm, pout_hbm, parts,
-    acts, gate_pre, up_pre, hidden_grad, proj_in, proj_out, gate_grad, up_grad, sems,
+    acts, gate_pre, up_pre, hidden_grad, proj_in, proj_out, sems,
 ):
     def fetch(at, which, source, target):
         copy = pltpu.make_async_copy(source, target, sems.at[at, which])
@@ -34,68 +35,134 @@
         return copy
 
     spans = [pl.ds(lo, hi - lo) for lo, hi in zip(cuts[:-1], cuts[1:], strict=True)]
-    waits = []
+    waits, rest = [], []
     for at, span in enumerate(spans):
         waits.append(
             [
                 fetch(at, 0, gate_hbm.at[:, span], gate_pre.at[:, span]),
                 fetch(at, 1, grad_hbm.at[:, span], hidden_grad.at[:, span]),
                 fetch(at, 2, up_hbm.at[:, span], up_pre.at[:, span]),
-                fetch(at, 3, pout_hbm.at[:, :, span], proj_out.at[:, :, span]),
             ]
         )
-    last = [
-        fetch(len(spans), 0, acts_hbm, acts),
-        fetch(len(spans), 1, pin_hbm, proj_in),
-    ]
+        if at == 0:
+            rest.append(fetch(at, 3, pout_hbm, proj_out))
+            rest.append(fetch(len(spans), 0, acts_hbm, acts))
+            rest.append(fetch(len(spans), 1, pin_hbm, proj_in))
     tok = gate_pre.shape[0]
-    total = None
+    rank = proj_in.shape[0]
+    tall, half = rank // n_x, rank // 2
+    tall_rows = range(0, tok, 64)
+    total = [None] * len(tall_rows)
     for at, (lo, hi) in enumerate(zip(cuts[:-1], cuts[1:], strict=True)):
         for copy in waits[at]:
             copy.wait()
         for col in range(lo, hi, 256):
             cols = slice(col, col + 256)
-            for row in range(0, tok, 32):
-                rows = slice(row, row + 32)
+            for k, row in enumerate(tall_rows):
+                rows = slice(row, row + 64)
                 gate = gate_pre[rows, cols].astype(jnp.float32)
                 sig = 0.5 * jnp.tanh(0.5 * gate) + 0.5
                 scaled = hidden_grad[rows, cols].astype(jnp.float32) * sig
-                up_grad[rows, cols] = (scaled * gate).astype(jnp.bfloat16)
+                up_grad = (scaled * gate).astype(jnp.bfloat16)
                 slope = 1.0 + gate * (1.0 - sig)
                 full = scaled * up_pre[rows, cols].astype(jnp.float32) * slope
-                gate_grad[rows, cols] = full.astype(jnp.bfloat16)
-            term = contract(proj_out[0, :, cols], gate_grad[:, cols])
-            term += contract(proj_out[1, :, cols], up_grad[:, cols])
-            total = term if total is None else total + term
-    for copy in last:
-        copy.wait()
-    ins = contract(proj_in[...], acts[...]).astype(jnp.bfloat16)
-    outs = total.astype(jnp.bfloat16)
-    rank = outs.shape[0]
-    tall, half = rank // n_x, rank // 2
-    for x in range(n_x):
-        for core in range(2):
-            slot = core * n_x + x
-            parts[slot, :tall] = outs[x * tall : (x + 1) * tall]
-            parts[slot, tall:] = ins[core * half : (core + 1) * half]
+                gate_grad = full.astype(jnp.bfloat16)
+                if col == 0 and row == 0:
+                    for copy in rest:
+                        copy.wait()
+                term = contract(gate_grad, proj_out[0, :, cols])
+                term += contract(up_grad, proj_out[1, :, cols])
+                total[k] = term if total[k] is None else total[k] + term
+        if at == 0:
+            ins = contract(proj_in[...], acts[...]).astype(jnp.bfloat16)
+            for slot in range(2 * n_x):
+                core = slot // n_x
+                parts[slot, tall:] = ins[core * half : (core + 1) * half]
+    outs = jnp.concatenate(total, axis=0).T.astype(jnp.bfloat16)
+    for slot in range(2 * n_x):
+        x = slot % n_x
+        parts[slot, :tall] = outs[x * tall : (x + 1) * tall]
 
 
 def project(n_x, acts, gate_pre, up_pre, hidden_grad, proj_in, proj_out):
     tok, hidden = gate_pre.shape
     rank = proj_in.shape[0]
-    cuts = (0,) + tuple(range(256, hidden + 1, 512))
+    cuts = (0, 512, 1024, hidden)
     shape = (2 * n_x, rank // n_x + rank // 2, tok)
     given = (acts, gate_pre, up_pre, hidden_grad, proj_in, proj_out)
     held = [pltpu.VMEM(a.shape, a.dtype) for a in given]
-    grads = [pltpu.VMEM((tok, hidden), jnp.bfloat16)] * 2
     return pl.pallas_call(
         functools.partial(project_kernel, n_x, cuts),
         in_specs=[pl.BlockSpec(memory_space=pltpu.HBM)] * len(given),
         out_specs=pl.BlockSpec(memory_space=pltpu.VMEM),
         out_shape=pltpu.VMEM(shape, jnp.bfloat16),
-        scratch_shapes=held + grads + [pltpu.SemaphoreType.DMA((len(cuts), 4))],
+        scratch_shapes=held + [pltpu.SemaphoreType.DMA((len(cuts), 4))],
         compiler_params=pltpu.CompilerParams(vmem_limit_bytes=VMEM),
     )(*[pltpu.with_memory_space_constraint(a, pltpu.HBM) for a in given])
+
+
+def turn_kernel(wide, got, near, away):
+    total = got[0].astype(jnp.float32)
+    for slot in range(1, got.shape[0]):
+        total += got[slot].astype(jnp.float32)
+    first = lax.axis_index("half") == 0
+    one, two, ins = total[:wide], total[wide : 2 * wide], total[2 * wide :]
+    near[...] = jnp.concatenate([jnp.where(first, one, two), ins], axis=0)
+    theirs = jnp.concatenate([jnp.where(first, two, one), ins], axis=0)
+    away[...] = theirs.astype(jnp.bfloat16)
+
+
+def turn(wide, got):
+    vmem = pl.BlockSpec(memory_space=pltpu.VMEM)
+    shape = (got.shape[1] - wide, got.shape[2])
+    return pl.pallas_call(
+        functools.partial(turn_kernel, wide),
+        in_specs=[vmem],
+        out_specs=[vmem, vmem],
+        out_shape=[
+            pltpu.VMEM(shape, jnp.float32),
+            jax.ShapeDtypeStruct(shape, jnp.bfloat16),
+        ],
+        compiler_params=pltpu.CompilerParams(vmem_limit_bytes=VMEM),
+    )(got)
+
+
+def outer_kernel(wide, near, far, sends):
+    total = near[...] + far[...].astype(jnp.float32)
+    outs, ins = total[:wide], total[wide:]
+    seqs, few = sends.shape[1], wide // 2
+    blocks = []
+    for seq in range(seqs):
+        cols = slice(seq * SEQ_LEN, (seq + 1) * SEQ_LEN)
+        blocks.append(
+            lax.dot_general(
+                outs[:, cols],
+                ins[:, cols],
+                (((1,), (1,)), ((), ())),
+                precision=lax.Precision.HIGHEST,
+                preferred_element_type=jnp.float32,
+            )
+        )
+    n_peer = sends.shape[0] // 2
+    for core in range(2):
+        lines = []
+        for block in blocks:
+            rows = [block[core * few + a : core * few + a + 1] for a in range(few)]
+            lines.append(jnp.concatenate(rows, axis=1))
+        pair = jnp.concatenate(lines, axis=0)[None]
+        pair = jnp.broadcast_to(pair, (n_peer, seqs, pair.shape[2]))
+        sends[core * n_peer : (core + 1) * n_peer] = pair.astype(jnp.bfloat16)
+
+
+def outer_blocks(wide, shape, near, far):
+    vmem = pl.BlockSpec(memory_space=pltpu.VMEM)
+    return pl.pallas_call(
+        functools.partial(outer_kernel, wide),
+        in_specs=[vmem, vmem],
+        out_specs=vmem,
+        out_shape=pltpu.VMEM(shape, jnp.bfloat16),
+        compiler_params=pltpu.CompilerParams(vmem_limit_bytes=VMEM),
+    )(near, far)
 
 
 def score_kernel(n_x, blocks, place, queries, part):
@@ -128,7 +195,8 @@
     n_seq = blocks.shape[1]
     row = lax.broadcasted_iota(jnp.int32, (8, n_seq), 0)
     seq = lax.broadcasted_iota(jnp.int32, (8, n_seq), 1)
-    pick = (seq == lax.axis_index("dp") * seqs + row).astype(jnp.bfloat16)
+    seat = lax.axis_index("y") * lax.axis_size("low") + lax.axis_index("low")
+    pick = (seq == seat * seqs + row).astype(jnp.bfloat16)
     total = None
     for side in range(2):
         lines = jnp.dot(pick, blocks[side], preferred_element_type=jnp.float32)
@@ -181,23 +249,17 @@
     rank = proj_in.shape[0]
     tok = acts.shape[0]
     seqs = tok // SEQ_LEN
-    n_dp, n_x = lax.axis_size("dp"), lax.axis_size("x")
+    n_y, n_low, n_x = lax.axis_size("y"), lax.axis_size("low"), lax.axis_size("x")
     tall = rank // n_x
     wide = tall // 2
     few = wide // 2
     half = rank // 2
     parts = project(n_x, acts, gate_pre, up_pre, hidden_grad, proj_in, proj_out)
-    near = jnp.sum(exchange(parts, ("core", "x")).astype(jnp.float32), axis=0)
-    far = lax.ppermute(near.astype(jnp.bfloat16), "half", SWAP)
-    total = near + far.astype(jnp.float32)
-    outs = lax.dynamic_slice_in_dim(total, lax.axis_index("half") * wide, wide, 0)
-    outs = outs.reshape(wide, seqs, SEQ_LEN)
-    ins = total[tall:].reshape(half, seqs, SEQ_LEN)
-    block = jnp.einsum("ast,bst->sab", outs, ins, precision=lax.Precision.HIGHEST)
-    block = block.astype(jnp.bfloat16).reshape(seqs, 2, few * half)
-    sends = jnp.broadcast_to(block.transpose(1, 0, 2)[:, None], (2, n_dp, seqs, few * half))
-    sends = sends.reshape(2 * n_dp, seqs, few * half)
-    got = exchange(sends, ("core", "dp")).reshape(2, n_dp * seqs, few * half)
+    near, away = turn(wide, exchange(parts, ("core", "x")))
+    far = lax.ppermute(away, "half", SWAP)
+    sends = outer_blocks(wide, (2 * n_y * n_low, seqs, few * half), near, far)
+    got = exchange(sends, ("core", "y", "low"))
+    got = got.reshape(2, n_y * n_low * seqs, few * half)
     src = np.arange(few * half)[:, None]
     dst = src // half * rank + src % half
     col = np.arange(few * rank)[None, :]
@@ -213,19 +275,20 @@
 
 def solution(mesh):
     n_dp, n_tensor = mesh.devices.shape
-    fine = Mesh(mesh.devices.reshape(n_dp, n_tensor // 4, 2, 2), ("dp",) + COLS)
+    fine = mesh.devices.reshape(n_dp // 8, 8, n_tensor // 4, 2, 2)
+    fine = Mesh(fine, DP + COLS)
     return jax.shard_map(
         per_device,
         mesh=fine,
         in_specs=(
-            P("dp", COLS),
-            P("dp", COLS),
-            P("dp", COLS),
-            P("dp", COLS),
+            P(DP, COLS),
+            P(DP, COLS),
+            P(DP, COLS),
+            P(DP, COLS),
             P(None, COLS),
             P(None, None, COLS),
-            P("dp", COLS),
+            P(DP, COLS),
         ),
-        out_specs=(P("dp", COLS), P(("dp",) + COLS, None)),
+        out_specs=(P(DP, COLS), P(DP + COLS, None)),
         check_vma=False,
     )

time: 82.6 us -> 82.4 us (level)
  no operation moved by 1% of the time
where the time goes in v5:
time: 82.4 us; the launch traced here: 82.1 us
  blocking collectives  50.5 us (61%)
  starting transfers between devices  19.8 us (24%)
  waiting for transfers between devices  5.9 us (7%)
  Pallas kernels  4.5 us (5%)
    all_to_all x3, blocking collectives, exchange(): lax.all_to_all(blocks, axes, split_axis=0, concat_axis=0, tiled=False)  50.5 us
    ppermute x1, starting transfers between devices, per_device(): far = lax.ppermute(away, 'half', SWAP)  11.9 us
    ppermute x1, starting transfers between devices, per_device(): far = lax.ppermute(theirs, 'half', SWAP)  7.94 us
    ppermute x1, waiting for transfers between devices, per_device(): far = lax.ppermute(theirs, 'half', SWAP)  4.44 us
    pallas_call x1, Pallas kernels, project(): pl.pallas_call(functools.partial(project_kernel, n_x, cuts), in_specs=[pl...  2.85 us
  transfers between devices with their start and end apart: 2, of which 2 were waited for; matrix products, arithmetic and copies ran while one was open for 0% of the time, Pallas kernels for 1%

profile of v5, /device:TPU:1, one launch (start us, length us, event | category | flops | bytes accessed | tf_op | source)
XLA Modules:
  0.0 82.1 jit_solution(5348387379233515200)
XLA Ops:
  0.6 0.0 copy-start
  0.6 2.8 %shard_map.95 = bf16[8,48,256]{2,1,0:T(8,128)(2,1)S(1)} custom-call(bf16[256,512]{1,0:T(8,128)(2,1)} %acts_hbm.1, bf16[256,1792]{1,0:T(8,128)(2,1)} %gate_hbm.1, bf16[256,1792]{1,0:T(8,128)(2,1)} %up_hbm.1, bf16[256,1792]{1,0:T(8,128)(2,1)} %grad_hbm.1, bf16[64,512]{1,0:T(8,128)(2,1)} %pin_hbm.1, bf16[2,64,1792]{2,1,0:T(8,128)(2,1)} %pout_hbm.1), custom_call_target="tpu_custom_call" | custom-call | tf_op jit(solution)/shard_map/pallas_call | solution.py:94
  3.5 15.2 %all_to_all.15.got = bf16[8,48,256]{2,1,0:T(8,128)(2,1)S(1)} all-to-all(bf16[8,48,256]{2,1,0:T(8,128)(2,1)S(1)} %shard_map.95), channel_id=1, replica_groups=mesh['y'=4,'low'=8,'x'=4,'half'=2,'core'=2] {'core','x'}, dimensions={0} | all-to-all | bytes 393216 | tf_op jit(solution)/shard_map/all_to_all | solution.py:25
  18.7 0.0 copy-start.1
  18.7 11.9 %collective-permute-start = (bf16[40,256]{1,0:T(8,128)(2,1)S(1)}, bf16[40,256]{1,0:T(8,128)(2,1)S(1)}, u32[]{:S(2)}, u32[]{:S(2)}) collective-permute-start(bf16[40,256]{1,0:T(8,128)(2,1)S(1)} %get-tuple-element.9), channel_id=1, source_target_pairs={{0,2},{2,0},{1,3},{3,1},{4,6},{6,4},{5,7},{7,5},{8,10},{10,8},{9,1... | collective-permute-start | bytes 61448 | tf_op jit(solution)/shard_map/ppermute | solution.py:259
  30.6 1.5 %collective-permute-done.far = bf16[40,256]{1,0:T(8,128)(2,1)S(1)} collective-permute-done((bf16[40,256]{1,0:T(8,128)(2,1)S(1)}, bf16[40,256]{1,0:T(8,128)(2,1)S(1)}, u32[]{:S(2)}, u32[]{:S(2)}) %collective-permute-start) | collective-permute-done | bytes 20512 | tf_op jit(solution)/shard_map/ppermute | solution.py:259
  32.1 0.3 shard_map.97
  32.3 25.2 %all_to_all.16 = bf16[64,2,128]{2,1,0:T(2,128)(2,1)S(1)} all-to-all(bf16[64,2,128]{2,1,0:T(2,128)(2,1)S(1)} %shard_map.97), channel_id=1, replica_groups=mesh['y'=4,'low'=8,'x'=4,'half'=2,'core'=2] {'core','y','low'}, dimensions={0} | all-to-all | bytes 65536 | tf_op jit(solution)/shard_map/all_to_all | solution.py:25
  57.5 0.0 copy-done
  57.5 0.0 copy-done.1
  57.5 0.5 shard_map.98
  58.0 10.2 %all_to_all.17.got = bf16[8,2,64,128]{3,2,1,0:T(8,128)(2,1)S(1)} all-to-all(bf16[8,2,64,128]{3,2,1,0:T(8,128)(2,1)S(1)} %shard_map.98), channel_id=1, replica_groups=mesh['y'=4,'low'=8,'x'=4,'half'=2,'core'=2] {'core','x'}, dimensions={0} | all-to-all | bytes 524288 | tf_op jit(solution)/shard_map/all_to_all | solution.py:25
  68.3 7.9 %collective-permute-start.1 = (bf16[64,128]{1,0:T(8,128)(2,1)S(1)}, bf16[64,128]{1,0:T(8,128)(2,1)S(1)}, u32[]{:S(2)}, u32[]{:S(2)}) collective-permute-start(bf16[64,128]{1,0:T(8,128)(2,1)S(1)} %get-tuple-element.13), channel_id=1, source_target_pairs={{0,2},{2,0},{1,3},{3,1},{4,6},{6,4},{5,7},{7,5},{8,10},{10,8},{9,1... | collective-permute-start | bytes 49160 | tf_op jit(solution)/shard_map/ppermute | solution.py:270
  76.2 0.8 shard_map.100
  77.0 4.4 %collective-permute-done.1 = bf16[64,128]{1,0:T(8,128)(2,1)S(1)} collective-permute-done((bf16[64,128]{1,0:T(8,128)(2,1)S(1)}, bf16[64,128]{1,0:T(8,128)(2,1)S(1)}, u32[]{:S(2)}, u32[]{:S(2)}) %collective-permute-start.1) | collective-permute-done | bytes 16416 | tf_op jit(solution)/shard_map/ppermute | solution.py:270
  81.5 0.6 add_bitcast_fusion
  (2 shorter events, 0.1 us)
Async XLA Ops:
  0.6 56.9 %copy-start = (bf16[2048,256]{1,0:T(8,128)(2,1)S(1)}, bf16[2048,256]{1,0:T(8,128)(2,1)}, u32[]{:S(2)}) copy-start(bf16[2048,256]{1,0:T(8,128)(2,1)} %queries.1) | copy-start | bytes 3145732
  18.7 38.8 %copy-start.1 = (bf16[2,128,256]{2,1,0:T(8,128)(2,1)S(1)}, bf16[2,128,256]{2,1,0:T(8,128)(2,1)}, u32[]{:S(2)}) copy-start(bf16[2,128,256]{2,1,0:T(8,128)(2,1)} %constant.2.clone.place) | copy-start | bytes 393220
  18.7 13.4 %collective-permute-start = (bf16[40,256]{1,0:T(8,128)(2,1)S(1)}, bf16[40,256]{1,0:T(8,128)(2,1)S(1)}, u32[]{:S(2)}, u32[]{:S(2)}) collective-permute-start(bf16[40,256]{1,0:T(8,128)(2,1)S(1)} %get-tuple-element.9), channel_id=1, source_target_pairs={{0,2},{2,0},{1,3},{3,1},{4,6},{6,4},{5,7},{7,5},{8,10},{10,8},{9,1... | collective-permute-start | bytes 61448 | tf_op jit(solution)/shard_map/ppermute | solution.py:259
  68.3 13.2 %collective-permute-start.1 = (bf16[64,128]{1,0:T(8,128)(2,1)S(1)}, bf16[64,128]{1,0:T(8,128)(2,1)S(1)}, u32[]{:S(2)}, u32[]{:S(2)}) collective-permute-start(bf16[64,128]{1,0:T(8,128)(2,1)S(1)} %get-tuple-element.13), channel_id=1, source_target_pairs={{0,2},{2,0},{1,3},{3,1},{4,6},{6,4},{5,7},{7,5},{8,10},{10,8},{9,1... | collective-permute-start | bytes 49160 | tf_op jit(solution)/shard_map/ppermute | solution.py:270

commit v6 on v5

--- a/solution.py
+++ b/solution.py
@@ -2,7 +2,6 @@
 
 import jax
 import jax.numpy as jnp
-import numpy as np
 from jax import lax
 from jax.experimental import pallas as pl
 from jax.experimental.pallas import tpu as pltpu
@@ -165,10 +164,16 @@
     )(near, far)
 
 
-def score_kernel(n_x, blocks, place, queries, part):
-    one = jnp.dot(blocks[0], place[0], preferred_element_type=jnp.float32)
-    two = jnp.dot(blocks[1], place[1], preferred_element_type=jnp.float32)
-    train = (one + two).astype(jnp.bfloat16)
+def interleave(few, blocks):
+    half = blocks.shape[2] // few
+    spans = [slice(at * half, (at + 1) * half) for at in range(few)]
+    return jnp.concatenate(
+        [blocks[side, :, span] for span in spans for side in range(2)], axis=1
+    )
+
+
+def score_kernel(n_x, few, blocks, queries, part):
+    train = interleave(few, blocks)
     rows = part.shape[3]
     for x in range(n_x):
         for half in range(2):
@@ -178,43 +183,38 @@
             part[n_x + x, half] = both[:, rows:]
 
 
-def partial_scores(n_x, blocks, place, queries):
+def partial_scores(n_x, few, blocks, queries):
     n_seq = blocks.shape[1]
     rows = queries.shape[0] // (4 * n_x)
     vmem = pl.BlockSpec(memory_space=pltpu.VMEM)
     return pl.pallas_call(
-        functools.partial(score_kernel, n_x),
-        in_specs=[vmem, vmem, vmem],
+        functools.partial(score_kernel, n_x, few),
+        in_specs=[vmem, vmem],
         out_specs=vmem,
         out_shape=pltpu.VMEM((2 * n_x, 2, n_seq, rows), jnp.bfloat16),
         compiler_params=pltpu.CompilerParams(vmem_limit_bytes=VMEM),
-    )(blocks, place, queries)
-
-
-def own_kernel(seqs, blocks, place, sketches):
+    )(blocks, queries)
+
+
+def own_kernel(seqs, few, blocks, sketches):
     n_seq = blocks.shape[1]
     row = lax.broadcasted_iota(jnp.int32, (8, n_seq), 0)
     seq = lax.broadcasted_iota(jnp.int32, (8, n_seq), 1)
     seat = lax.axis_index("y") * lax.axis_size("low") + lax.axis_index("low")
     pick = (seq == seat * seqs + row).astype(jnp.bfloat16)
-    total = None
-    for side in range(2):
-        lines = jnp.dot(pick, blocks[side], preferred_element_type=jnp.float32)
-        lines = lines.astype(jnp.bfloat16)
-        term = jnp.dot(lines, place[side], preferred_element_type=jnp.float32)
-        total = term if total is None else total + term
+    total = jnp.dot(pick, interleave(few, blocks), preferred_element_type=jnp.float32)
     sketches[...] = total[:seqs].astype(jnp.bfloat16)
 
 
-def own_sketches(seqs, blocks, place):
-    vmem = pl.BlockSpec(memory_space=pltpu.VMEM)
-    return pl.pallas_call(
-        functools.partial(own_kernel, seqs),
-        in_specs=[vmem, vmem],
+def own_sketches(seqs, few, blocks):
+    vmem = pl.BlockSpec(memory_space=pltpu.VMEM)
+    return pl.pallas_call(
+        functools.partial(own_kernel, seqs, few),
+        in_specs=[vmem],
         out_specs=vmem,
-        out_shape=jax.ShapeDtypeStruct((seqs, place.shape[2]), jnp.bfloat16),
-        compiler_params=pltpu.CompilerParams(vmem_limit_bytes=VMEM),
-    )(blocks, place)
+        out_shape=jax.ShapeDtypeStruct((seqs, 2 * blocks.shape[2]), jnp.bfloat16),
+        compiler_params=pltpu.CompilerParams(vmem_limit_bytes=VMEM),
+    )(blocks)
 
 
 def split_kernel(got, mine, theirs):
@@ -260,15 +260,11 @@
     sends = outer_blocks(wide, (2 * n_y * n_low, seqs, few * half), near, far)
     got = exchange(sends, ("core", "y", "low"))
     got = got.reshape(2, n_y * n_low * seqs, few * half)
-    src = np.arange(few * half)[:, None]
-    dst = src // half * rank + src % half
-    col = np.arange(few * rank)[None, :]
-    place = np.stack([col == dst, col == dst + half]).astype(jnp.bfloat16)
-    part = partial_scores(n_x, got, place, queries)
+    part = partial_scores(n_x, few, got, queries)
     mine, theirs = split_scores(exchange(part, ("core", "x")))
     theirs, got = lax.optimization_barrier((theirs, got))
     far = lax.ppermute(theirs, "half", SWAP)
-    sketches = own_sketches(seqs, got, place)
+    sketches = own_sketches(seqs, few, got)
     scores = (mine + far.astype(jnp.float32)).T
     return (sketches, scores)
 

time: 82.4 us -> 82.2 us (level)
  no operation moved by 1% of the time
where the time goes in v6:
time: 82.2 us; the launch traced here: 81.9 us
  blocking collectives  50.5 us (61%)
  starting transfers between devices  19.7 us (24%)
  waiting for transfers between devices  5.93 us (7%)
  Pallas kernels  4.39 us (5%)
    all_to_all x3, blocking collectives, exchange(): lax.all_to_all(blocks, axes, split_axis=0, concat_axis=0, tiled=False)  50.5 us
    ppermute x1, starting transfers between devices, per_device(): far = lax.ppermute(away, 'half', SWAP)  11.8 us
    ppermute x1, starting transfers between devices, per_device(): far = lax.ppermute(theirs, 'half', SWAP)  7.94 us
    ppermute x1, waiting for transfers between devices, per_device(): far = lax.ppermute(theirs, 'half', SWAP)  4.48 us
    pallas_call x1, Pallas kernels, project(): pl.pallas_call(functools.partial(project_kernel, n_x, cuts), in_specs=[pl...  2.85 us
  transfers between devices with their start and end apart: 2, of which 2 were waited for; matrix products, arithmetic and copies ran while one was open for 0% of the time, Pallas kernels for 1%

profile of v6, /device:TPU:1, one launch (start us, length us, event | category | flops | bytes accessed | tf_op | source)
XLA Modules:
  0.0 81.9 jit_solution(15613977259406859628)
XLA Ops:
  0.6 0.0 copy-start
  0.6 2.8 %shard_map.86 = bf16[8,48,256]{2,1,0:T(8,128)(2,1)S(1)} custom-call(bf16[256,512]{1,0:T(8,128)(2,1)} %acts_hbm.1, bf16[256,1792]{1,0:T(8,128)(2,1)} %gate_hbm.1, bf16[256,1792]{1,0:T(8,128)(2,1)} %up_hbm.1, bf16[256,1792]{1,0:T(8,128)(2,1)} %grad_hbm.1, bf16[64,512]{1,0:T(8,128)(2,1)} %pin_hbm.1, bf16[2,64,1792]{2,1,0:T(8,128)(2,1)} %pout_hbm.1), custom_call_target="tpu_custom_call" | custom-call | tf_op jit(solution)/shard_map/pallas_call | solution.py:93
  3.5 15.2 %all_to_all.15.got = bf16[8,48,256]{2,1,0:T(8,128)(2,1)S(1)} all-to-all(bf16[8,48,256]{2,1,0:T(8,128)(2,1)S(1)} %shard_map.86), channel_id=1, replica_groups=mesh['y'=4,'low'=8,'x'=4,'half'=2,'core'=2] {'core','x'}, dimensions={0} | all-to-all | bytes 393216 | tf_op jit(solution)/shard_map/all_to_all | solution.py:24
  18.7 11.8 %collective-permute-start = (bf16[40,256]{1,0:T(8,128)(2,1)S(1)}, bf16[40,256]{1,0:T(8,128)(2,1)S(1)}, u32[]{:S(2)}, u32[]{:S(2)}) collective-permute-start(bf16[40,256]{1,0:T(8,128)(2,1)S(1)} %get-tuple-element.9), channel_id=1, source_target_pairs={{0,2},{2,0},{1,3},{3,1},{4,6},{6,4},{5,7},{7,5},{8,10},{10,8},{9,1... | collective-permute-start | bytes 61448 | tf_op jit(solution)/shard_map/ppermute | solution.py:259
  30.5 1.5 %collective-permute-done.far = bf16[40,256]{1,0:T(8,128)(2,1)S(1)} collective-permute-done((bf16[40,256]{1,0:T(8,128)(2,1)S(1)}, bf16[40,256]{1,0:T(8,128)(2,1)S(1)}, u32[]{:S(2)}, u32[]{:S(2)}) %collective-permute-start) | collective-permute-done | bytes 20512 | tf_op jit(solution)/shard_map/ppermute | solution.py:259
  31.9 0.3 shard_map.88
  32.2 25.2 %all_to_all.16 = bf16[64,2,128]{2,1,0:T(2,128)(2,1)S(1)} all-to-all(bf16[64,2,128]{2,1,0:T(2,128)(2,1)S(1)} %shard_map.88), channel_id=1, replica_groups=mesh['y'=4,'low'=8,'x'=4,'half'=2,'core'=2] {'core','y','low'}, dimensions={0} | all-to-all | bytes 65536 | tf_op jit(solution)/shard_map/all_to_all | solution.py:24
  57.4 0.0 copy-done
  57.4 0.4 shard_map.89
  57.8 10.2 %all_to_all.17.got = bf16[8,2,64,128]{3,2,1,0:T(8,128)(2,1)S(1)} all-to-all(bf16[8,2,64,128]{3,2,1,0:T(8,128)(2,1)S(1)} %shard_map.89), channel_id=1, replica_groups=mesh['y'=4,'low'=8,'x'=4,'half'=2,'core'=2] {'core','x'}, dimensions={0} | all-to-all | bytes 524288 | tf_op jit(solution)/shard_map/all_to_all | solution.py:24
  68.1 7.9 %collective-permute-start.1 = (bf16[64,128]{1,0:T(8,128)(2,1)S(1)}, bf16[64,128]{1,0:T(8,128)(2,1)S(1)}, u32[]{:S(2)}, u32[]{:S(2)}) collective-permute-start(bf16[64,128]{1,0:T(8,128)(2,1)S(1)} %get-tuple-element.13), channel_id=1, source_target_pairs={{0,2},{2,0},{1,3},{3,1},{4,6},{6,4},{5,7},{7,5},{8,10},{10,8},{9,1... | collective-permute-start | bytes 49160 | tf_op jit(solution)/shard_map/ppermute | solution.py:266
  76.0 0.8 shard_map.91
  76.8 4.5 %collective-permute-done.1 = bf16[64,128]{1,0:T(8,128)(2,1)S(1)} collective-permute-done((bf16[64,128]{1,0:T(8,128)(2,1)S(1)}, bf16[64,128]{1,0:T(8,128)(2,1)S(1)}, u32[]{:S(2)}, u32[]{:S(2)}) %collective-permute-start.1) | collective-permute-done | bytes 16416 | tf_op jit(solution)/shard_map/ppermute | solution.py:266
  81.3 0.6 add_bitcast_fusion
  (2 shorter events, 0.1 us)
Async XLA Ops:
  0.6 56.7 %copy-start = (bf16[2048,256]{1,0:T(8,128)(2,1)S(1)}, bf16[2048,256]{1,0:T(8,128)(2,1)}, u32[]{:S(2)}) copy-start(bf16[2048,256]{1,0:T(8,128)(2,1)} %queries.1) | copy-start | bytes 3145732
  18.7 13.2 %collective-permute-start = (bf16[40,256]{1,0:T(8,128)(2,1)S(1)}, bf16[40,256]{1,0:T(8,128)(2,1)S(1)}, u32[]{:S(2)}, u32[]{:S(2)}) collective-permute-start(bf16[40,256]{1,0:T(8,128)(2,1)S(1)} %get-tuple-element.9), channel_id=1, source_target_pairs={{0,2},{2,0},{1,3},{3,1},{4,6},{6,4},{5,7},{7,5},{8,10},{10,8},{9,1... | collective-permute-start | bytes 61448 | tf_op jit(solution)/shard_map/ppermute | solution.py:259
  68.1 13.2 %collective-permute-start.1 = (bf16[64,128]{1,0:T(8,128)(2,1)S(1)}, bf16[64,128]{1,0:T(8,128)(2,1)S(1)}, u32[]{:S(2)}, u32[]{:S(2)}) collective-permute-start(bf16[64,128]{1,0:T(8,128)(2,1)S(1)} %get-tuple-element.13), channel_id=1, source_target_pairs={{0,2},{2,0},{1,3},{3,1},{4,6},{6,4},{5,7},{7,5},{8,10},{10,8},{9,1... | collective-permute-start | bytes 49160 | tf_op jit(solution)/shard_map/ppermute | solution.py:266
